TPU v7x, 32 devices: a whole 2x2x4 slice. The times are simulated.
32 devices in a mesh: dp: 8 (over z, x), tensor: 4 (over y, core).
Axes of the slice: x: 2, y: 2, z: 4, core: 2. Of those that a mesh axis runs over, the one named last changes fastest.
Arguments:
- hidden: bfloat16 [16384, 768], P(('dp', 'tensor')), may hold values from -6 to 6
- segment_ids: int32 [16, 1024], P('dp'), may hold values from 0 to 3, as said below
- norm1_gain: float32 [768], replicated, may hold values from 0.25 to 1.75
- norm1_bias: float32 [768], replicated, may hold values from -1.75 to 1.75
- w_qkv: bfloat16 [3, 768, 768], P(None, 'dp', 'tensor'), may hold values from -0.21875 to 0.21875
- qv_bias: float32 [2, 768], P(None, 'tensor'), may hold values from -2.5 to 2.5
- w_out: bfloat16 [768, 768], P('tensor', 'dp'), may hold values from -1.75 to 1.75
- out_bias: float32 [768], replicated, may hold values from -1.75 to 1.75
- norm2_gain: float32 [768], replicated, may hold values from 0.25 to 1.75
- norm2_bias: float32 [768], replicated, may hold values from -1.75 to 1.75
- w_up: bfloat16 [768, 3072], P('dp', 'tensor'), may hold values from -0.21875 to 0.21875
- up_bias: float32 [3072], P('tensor'), may hold values from -3 to 3
- w_down: bfloat16 [3072, 768], P('tensor', 'dp'), may hold values from -0.15625 to 0.15625
- down_bias: float32 [768], replicated, may hold values from -1.75 to 1.75
- cotangent: bfloat16 [16384, 768], P(('dp', 'tensor')), may hold values from -6 to 6
Outputs:
- output: bfloat16 [16384, 768], P(('dp', 'tensor'))
- grad_hidden: bfloat16 [16384, 768], P(('dp', 'tensor'))
- grad_norm1_gain: float32 [768], replicated
- grad_norm1_bias: float32 [768], replicated
- grad_w_qkv: float32 [3, 768, 768], P(None, 'dp', 'tensor')
- grad_qv_bias: float32 [2, 768], P(None, 'tensor')
- grad_w_out: float32 [768, 768], P('tensor', 'dp')
- grad_out_bias: float32 [768], replicated
- grad_norm2_gain: float32 [768], replicated
- grad_norm2_bias: float32 [768], replicated
- grad_w_up: float32 [768, 3072], P('dp', 'tensor')
- grad_up_bias: float32 [3072], P('tensor')
- grad_w_down: float32 [3072, 768], P('tensor', 'dp')
- grad_down_bias: float32 [768], replicated
Inputs may be any that keep to these rules, and one draw needn't show every extreme that they name: `segment_ids`: within a sequence the numbers never fall, and tokens of equal number form one document. In each group of 2 sequences on one index of dp, one sequence is a single document.
All inputs are finite; a program needn't handle non-finite values.
Results may differ from a plain program's by a relative error of at most 0.018.
Values may be sent and summed in bfloat16 or wider, within the bound.
No kernel may reach another device: no remote copies, remote signals or barrier semaphores. Data moves between devices by JAX's collectives and lax.ppermute only.
A program may use at most 128 MiB of HBM per device.

v0:
```python
from functools import partial

import jax
import jax.numpy as jnp
from jax import lax
from jax.sharding import PartitionSpec as P

HEAD_DIM = 64


def layer_norm(values, gain, bias):
    center = values - jnp.mean(values, -1, keepdims=True)
    spread = jnp.mean(center * center, -1, keepdims=True)
    return center * lax.rsqrt(spread + 1e-05) * gain + bias


def body(
    hidden,
    segment_ids,
    norm1_gain,
    norm1_bias,
    w_qkv,
    qv_bias,
    w_out,
    out_bias,
    norm2_gain,
    norm2_bias,
    w_up,
    up_bias,
    w_down,
    down_bias,
    cotangent,
):
    seq_local = segment_ids.shape[0]
    length = segment_ids.shape[1]
    block_rows = min(512, length)
    per_seq = length // block_rows
    count = seq_local * per_seq
    local_width = w_qkv.shape[2]
    heads_here = local_width // HEAD_DIM
    query_scale = HEAD_DIM ** (-0.5)
    positions = jnp.arange(length)
    full_qkv, full_out, full_up, full_down = (
        lax.all_gather(w_qkv, "dp", axis=1, tiled=True),
        lax.all_gather(w_out, "dp", axis=1, tiled=True),
        lax.all_gather(w_up, "dp", axis=0, tiled=True),
        lax.all_gather(w_down, "dp", axis=1, tiled=True),
    )
    inputs = hidden.astype(jnp.float32)
    norm1_out, norm1_pull = jax.vjp(layer_norm, inputs, norm1_gain, norm1_bias)
    rows_one = lax.all_gather(norm1_out.astype(jnp.bfloat16), "tensor", axis=0, tiled=True)
    proj = jnp.einsum("td,cde->cte", rows_one, full_qkv, preferred_element_type=jnp.float32)
    queries = ((proj[0] + qv_bias[0]) * query_scale).astype(jnp.bfloat16)
    keys = proj[1].astype(jnp.bfloat16)
    values = (proj[2] + qv_bias[1]).astype(jnp.bfloat16)

    def scores_of(number):
        sequence = number // per_seq
        offset = number % per_seq * block_rows
        anchor = sequence * length
        query_block = lax.dynamic_slice_in_dim(queries, anchor + offset, block_rows, 0)
        query_block = query_block.reshape(block_rows, heads_here, HEAD_DIM)
        key_rows = lax.dynamic_slice_in_dim(keys, anchor, length, 0).reshape(
            length, heads_here, HEAD_DIM
        )
        value_rows = lax.dynamic_slice_in_dim(values, anchor, length, 0).reshape(
            length, heads_here, HEAD_DIM
        )
        seg_row = lax.dynamic_index_in_dim(segment_ids, sequence, 0, keepdims=False)
        seg_block = lax.dynamic_slice_in_dim(seg_row, offset, block_rows, 0)
        causal = (offset + jnp.arange(block_rows))[:, None] >= positions[None, :]
        allowed = causal & (seg_block[:, None] == seg_row[None, :])
        scores = jnp.einsum(
            "qhe,khe->hqk", query_block, key_rows, preferred_element_type=jnp.float32
        )
        scores = jnp.where(allowed[None], scores, -1e30)
        return (scores, query_block, key_rows, value_rows, anchor, offset)

    def attend_forward(number):
        scores, query_block, key_rows, value_rows, anchor, offset = scores_of(number)
        top_score = jnp.max(scores, -1, keepdims=True)
        shifted = jnp.exp(scores - top_score)
        total = jnp.sum(shifted, -1, keepdims=True)
        probs = shifted / total
        result = jnp.einsum(
            "hqk,khe->qhe",
            probs.astype(jnp.bfloat16),
            value_rows,
            preferred_element_type=jnp.float32,
        )
        return (
            result.reshape(block_rows, local_width).astype(jnp.bfloat16),
            (top_score + jnp.log(total))[..., 0],
        )

    attended, log_totals = lax.map(attend_forward, jnp.arange(count))
    attended = attended.reshape(seq_local * length, local_width)
    partial_attn = jnp.dot(attended, full_out, preferred_element_type=jnp.float32)
    attn_total = lax.psum_scatter(
        partial_attn.astype(jnp.bfloat16), "tensor", scatter_dimension=0, tiled=True
    ).astype(jnp.float32)
    middle = inputs + attn_total + out_bias
    norm2_out, norm2_pull = jax.vjp(layer_norm, middle, norm2_gain, norm2_bias)
    rows_two = lax.all_gather(norm2_out.astype(jnp.bfloat16), "tensor", axis=0, tiled=True)
    upper = jnp.dot(rows_two, full_up, preferred_element_type=jnp.float32) + up_bias
    active, gelu_pull = jax.vjp(partial(jax.nn.gelu, approximate=False), upper)
    active_low = active.astype(jnp.bfloat16)
    partial_mlp = jnp.dot(active_low, full_down, preferred_element_type=jnp.float32)
    mlp_total = lax.psum_scatter(
        partial_mlp.astype(jnp.bfloat16), "tensor", scatter_dimension=0, tiled=True
    ).astype(jnp.float32)
    output = (middle + mlp_total + down_bias).astype(jnp.bfloat16)
    grad_output = cotangent.astype(jnp.float32)
    grad_down_local = jnp.sum(grad_output, 0)
    grad_rows_two = lax.all_gather(cotangent, "tensor", axis=0, tiled=True)
    grad_w_down_full = jnp.einsum(
        "tf,td->fd", active_low, grad_rows_two, preferred_element_type=jnp.float32
    )
    grad_active = jnp.einsum(
        "td,fd->tf", grad_rows_two, full_down, preferred_element_type=jnp.float32
    )
    grad_upper = gelu_pull(grad_active)[0].astype(jnp.bfloat16)
    grad_up_local = jnp.sum(grad_upper.astype(jnp.float32), 0)
    grad_w_up_full = jnp.einsum(
        "td,tf->df", rows_two, grad_upper, preferred_element_type=jnp.float32
    )
    partial_norm2 = jnp.einsum("tf,df->td", grad_upper, full_up, preferred_element_type=jnp.float32)
    grad_normed2 = lax.psum_scatter(
        partial_norm2.astype(jnp.bfloat16), "tensor", scatter_dimension=0, tiled=True
    ).astype(jnp.float32)
    grad_mid_norm, grad_gain2, grad_bias2 = norm2_pull(grad_normed2)
    grad_middle = grad_output + grad_mid_norm
    grad_attn = grad_middle.astype(jnp.bfloat16)
    grad_out_local = jnp.sum(grad_attn.astype(jnp.float32), 0)
    grad_rows_one = lax.all_gather(grad_attn, "tensor", axis=0, tiled=True)
    grad_w_out_full = jnp.einsum(
        "te,td->ed", attended, grad_rows_one, preferred_element_type=jnp.float32
    )
    grad_attended = jnp.einsum(
        "td,ed->te", grad_rows_one, full_out, preferred_element_type=jnp.float32
    ).astype(jnp.bfloat16)

    def attend_backward(carry, number):
        grad_keys, grad_values = carry
        scores, query_block, key_rows, value_rows, anchor, offset = scores_of(number)
        probs = jnp.exp(scores - log_totals[number][..., None])
        grad_block = lax.dynamic_slice_in_dim(grad_attended, anchor + offset, block_rows, 0)
        grad_block = grad_block.reshape(block_rows, heads_here, HEAD_DIM)
        grad_probs = jnp.einsum(
            "qhe,khe->hqk", grad_block, value_rows, preferred_element_type=jnp.float32
        )
        inner = jnp.sum(probs * grad_probs, -1, keepdims=True)
        grad_scores = (probs * (grad_probs - inner)).astype(jnp.bfloat16)
        grad_query = jnp.einsum(
            "hqk,khe->qhe", grad_scores, key_rows, preferred_element_type=jnp.float32
        )
        key_part = jnp.einsum(
            "hqk,qhe->khe", grad_scores, query_block, preferred_element_type=jnp.float32
        )
        value_part = jnp.einsum(
            "hqk,qhe->khe",
            probs.astype(jnp.bfloat16),
            grad_block,
            preferred_element_type=jnp.float32,
        )
        old_keys = lax.dynamic_slice_in_dim(grad_keys, anchor, length, 0)
        grad_keys = lax.dynamic_update_slice_in_dim(
            grad_keys, old_keys + key_part.reshape(length, local_width), anchor, 0
        )
        old_values = lax.dynamic_slice_in_dim(grad_values, anchor, length, 0)
        grad_values = lax.dynamic_update_slice_in_dim(
            grad_values, old_values + value_part.reshape(length, local_width), anchor, 0
        )
        return ((grad_keys, grad_values), grad_query.reshape(block_rows, local_width))

    empty = jnp.zeros((seq_local * length, local_width), jnp.float32)
    (grad_keys, grad_values), grad_queries = lax.scan(
        attend_backward, (empty, empty), jnp.arange(count)
    )
    grad_queries = (
        grad_queries.reshape(seq_local * length, local_width).astype(jnp.bfloat16) * query_scale
    )
    grad_stack = jnp.stack(
        [grad_queries, grad_keys.astype(jnp.bfloat16), grad_values.astype(jnp.bfloat16)]
    )
    grad_qkv_full = jnp.einsum(
        "td,cte->cde", rows_one, grad_stack, preferred_element_type=jnp.float32
    )
    grad_qv_local = jnp.stack(
        [
            jnp.sum(grad_stack[0].astype(jnp.float32), 0),
            jnp.sum(grad_stack[2].astype(jnp.float32), 0),
        ]
    )
    partial_norm1 = jnp.einsum(
        "cte,cde->td", grad_stack, full_qkv, preferred_element_type=jnp.float32
    )
    grad_normed1 = lax.psum_scatter(
        partial_norm1.astype(jnp.bfloat16), "tensor", scatter_dimension=0, tiled=True
    ).astype(jnp.float32)
    grad_input_norm, grad_gain1, grad_bias1 = norm1_pull(grad_normed1)
    grad_hidden = (grad_middle + grad_input_norm).astype(jnp.bfloat16)
    grad_w_qkv, grad_w_out, grad_w_up, grad_w_down = (
        lax.psum_scatter(grad_qkv_full, "dp", scatter_dimension=1, tiled=True),
        lax.psum_scatter(grad_w_out_full, "dp", scatter_dimension=1, tiled=True),
        lax.psum_scatter(grad_w_up_full, "dp", scatter_dimension=0, tiled=True),
        lax.psum_scatter(grad_w_down_full, "dp", scatter_dimension=1, tiled=True),
    )
    gain_one, bias_one, grad_out_bias, gain_two, bias_two, grad_down_bias = lax.psum(
        (grad_gain1, grad_bias1, grad_out_local, grad_gain2, grad_bias2, grad_down_local),
        ("dp", "tensor"),
    )
    grad_qv_bias, grad_up_bias = lax.psum((grad_qv_local, grad_up_local), "dp")
    return (
        output,
        grad_hidden,
        gain_one,
        bias_one,
        grad_w_qkv,
        grad_qv_bias,
        grad_w_out,
        grad_out_bias,
        gain_two,
        bias_two,
        grad_w_up,
        grad_up_bias,
        grad_w_down,
        grad_down_bias,
    )


def solution(mesh):
    placed = (
        P(("dp", "tensor"), None),
        P("dp", None),
        P(),
        P(),
        P(None, "dp", "tensor"),
        P(None, "tensor"),
        P("tensor", "dp"),
        P(),
        P(),
        P(),
        P("dp", "tensor"),
        P("tensor"),
        P("tensor", "dp"),
        P(),
        P(("dp", "tensor"), None),
    )
    return jax.shard_map(
        body,
        mesh=mesh,
        in_specs=placed,
        out_specs=(
            P(("dp", "tensor"), None),
            P(("dp", "tensor"), None),
            P(),
            P(),
            P(None, "dp", "tensor"),
            P(None, "tensor"),
            P("tensor", "dp"),
            P(),
            P(),
            P(),
            P("dp", "tensor"),
            P("tensor"),
            P("tensor", "dp"),
            P(),
        ),
        check_vma=False,
    )
```

profile of v0, /device:TPU:0, one launch (start us, length us, event | category | flops | bytes accessed | tf_op | source)
XLA Modules:
  0.0 784.0 jit_solution(9508412609497085640)
XLA Ops:
  11.0 2.4 fusion.34
  13.7 38.9 %all_gather.25 = bf16[3,768,192]{2,0,1:T(4,128)(2,1)S(1)} all-gather(bf16[3,96,192]{2,0,1:T(4,128)(2,1)S(1)} %copy.38), channel_id=1, replica_groups=mesh['dp'=8,'tensor'=4] {'dp'}, dimensions={1}, use_global_device_ids=true | all-gather | bytes 995328 | tf_op jit(solution)/shard_map/all_gather | solution.py:44
  53.5 31.2 %all_gather.26 = bf16[192,768]{0,1:T(8,128)(2,1)S(1)} all-gather(bf16[192,96]{0,1:T(8,128)(2,1)S(1)} %copy.41), channel_id=1, replica_groups=mesh['dp'=8,'tensor'=4] {'dp'}, dimensions={1}, use_global_device_ids=true | all-gather | bytes 331776 | tf_op jit(solution)/shard_map/all_gather | solution.py:45
  84.7 3.9 fusion.65
  89.4 40.3 %while.34 = (s32[]{:T(128)}, bf16[4,512,192]{1,2,0:T(8,128)(2,1)}, f32[4,3,512]{2,1,0:T(4,128)}, s32[4]{0:T(128)S(1)}, bf16[2048,192]{0,1:T(8,128)(2,1)S(1)}, /*...) while((s32[]{:T(128)}, bf16[4,512,192]{1,2,0:T(8,128)(2,1)}, ...), condition=%wide.region_5.6_spmd.clone, body=%wide.region_2.5_spmd.clone.sunk | while | flops 418479136 | bytes 24584772 | solution.py:96
  94.6 1.6 fusion.127
  96.1 2.0 fusion.128
  104.6 1.6 fusion.127
  106.2 2.0 fusion.128
  114.7 1.6 fusion.127
  116.3 2.0 fusion.128
  126.4 2.0 fusion.128
  129.7 1.8 copy.50
  132.4 2.7 convolution_convert_fusion.2
  135.8 36.8 %reduce-scatter.13.cloned.1.call-done = bf16[512,768]{1,0:T(8,128)(2,1)} async-done(((bf16[2048,768]{1,0:T(8,128)(2,1)}), bf16[512,768]{1,0:T(8,128)(2,1)}) %reduce-scatter.13.cloned.1.call-update) | async-done | bytes 786448 | tf_op jit(solution)/shard_map/reduce_scatter | solution.py:99
  175.8 2.0 add_convert_fusion.3
  179.2 10.4 %reduce-scatter.17.cloned.1.call-start = ((), (), s32[]{:S(2)}) async-start(), calls=%async_computation.15 | async-start | bytes 3932160 | tf_op jit(solution)/shard_map/reduce_scatter | solution.py:128
  189.6 18.3 %all-gather.9.cloned.1.call-done = bf16[2048,768]{1,0:T(8,128)(2,1)} async-done(((bf16[512,768]{1,0:T(8,128)(2,1)}), bf16[2048,768]{1,0:T(8,128)(2,1)}) %all-gather.9.cloned.1.call-update) | async-done | bytes 3145744 | tf_op jit(solution)/shard_map/all_gather | solution.py:104
  207.9 7.5 fusion.66
  215.4 36.4 %all-gather.13.cloned.1.call-done = bf16[768,768]{0,1:T(8,128)(2,1)} async-done(((bf16[768,96]{0,1:T(8,128)(2,1)}), bf16[768,768]{0,1:T(8,128)(2,1)}) %all-gather.13.cloned.1.call-update) | async-done | bytes 1179664 | tf_op jit(solution)/shard_map/all_gather | solution.py:47
  251.8 28.6 %all-gather.15.cloned.1.call-done = bf16[2048,768]{1,0:T(8,128)(2,1)} async-done(((bf16[512,768]{1,0:T(8,128)(2,1)}), bf16[2048,768]{1,0:T(8,128)(2,1)}) %all-gather.15.cloned.1.call-update) | async-done | bytes 3145744 | tf_op jit(solution)/shard_map/all_gather | solution.py:115
  280.3 20.6 %convert_reduce_fusion = (f32[768]{0:T(1024)}, bf16[2048,768]{1,0:T(8,128)(2,1)S(1)}, f32[2048,768]{1,0:T(8,128)}) fusion(f32[2048,768]{1,0:T(8,128)} %fusion.66, f32[768]{0:T(1024)S(1)} %copy-done.35, bf16[2048,768]{1,0:T(8,128)(2,1)} %all-gather.15.cloned.1.call-done, bf16[768,768]{0,1:T(8,128)(2,1)} %all-gather.13.cloned.1.call-done), kind=kOutput, calls=%fused_computation.44 | convolution fusion | flops 2533883136 | bytes 20060160 | tf_op jit(solution)/shard_map/td,fd->tf/dot_general | solution.py:119
  300.9 1.7 copy-done.41
  302.6 4.0 convolution_convert_fusion
  306.7 5.6 multiply_convert_fusion.1
  312.3 1.6 copy-done.10
  313.9 4.0 convolution_convert_fusion.1
  318.0 26.7 %reduce-scatter.17.cloned.1.call-done = bf16[512,768]{1,0:T(8,128)(2,1)} async-done(((bf16[2048,768]{1,0:T(8,128)(2,1)}), bf16[512,768]{1,0:T(8,128)(2,1)}) %reduce-scatter.17.cloned.1.call-update) | async-done | bytes 786448 | tf_op jit(solution)/shard_map/reduce_scatter | solution.py:128
  344.7 2.5 fusion.39
  348.6 36.5 %reduce-scatter.15.cloned.1.call-done = bf16[512,768]{1,0:T(8,128)(2,1)} async-done(((bf16[2048,768]{1,0:T(8,128)(2,1)}), bf16[512,768]{1,0:T(8,128)(2,1)}) %reduce-scatter.15.cloned.1.call-update) | async-done | bytes 786448 | tf_op jit(solution)/shard_map/reduce_scatter | solution.py:109
  385.1 3.2 fusion.60
  390.8 28.4 %all-gather.17.cloned.1.call-done = bf16[2048,768]{1,0:T(8,128)(2,1)} async-done(((bf16[512,768]{1,0:T(8,128)(2,1)}), bf16[2048,768]{1,0:T(8,128)(2,1)}) %all-gather.17.cloned.1.call-update) | async-done | bytes 3145744 | tf_op jit(solution)/shard_map/all_gather | solution.py:135
  419.3 4.1 convolution_bitcast_fusion
  423.5 4.0 convolution_convert_fusion.3
  428.9 79.2 %while.35 = (s32[]{:T(128)}, f32[2048,192]{0,1:T(8,128)S(1)}, f32[2048,192]{0,1:T(8,128)}, bf16[4,512,192]{1,2,0:T(8,128)(2,1)}, s32[4]{0:T(128)S(1)}, /*index=5...) while((s32[]{:T(128)}, f32[2048,192]{0,1:T(8,128)S(1)}, ...), condition=%wide.region_15.16_spmd.clone, body=%wide.region_13.15_spmd.clone.sunk | while | flops 1027472384 | bytes 73138880 | solution.py:177
  439.2 1.7 fusion.141
  440.9 2.4 multiply_reduce_fusion.3
  443.3 1.7 multiply_convert_fusion.3
  458.9 1.7 fusion.141
  460.6 2.4 multiply_reduce_fusion.3
  463.0 1.7 multiply_convert_fusion.3
  478.6 1.7 fusion.141
  480.3 2.4 multiply_reduce_fusion.3
  482.7 1.7 multiply_convert_fusion.3
  498.3 1.7 fusion.141
  500.0 2.4 multiply_reduce_fusion.3
  502.4 1.7 multiply_convert_fusion.3
  511.6 1.7 convert_reduce_fusion.6
  514.5 2.0 fusion.46
  516.5 2.7 copy.45
  519.3 4.9 reshape.392
  524.3 5.5 bitcast_convert_fusion
  529.8 7.2 fusion.68
  537.1 6.9 fusion.67
  544.1 22.6 %all-reduce.1 = (f32[2,192]{1,0:T(2,128)}, f32[768]{0:T(1024)}) all-reduce(f32[2,192]{1,0:T(2,128)S(1)} %pad_maximum_fusion.3, f32[768]{0:T(1024)S(1)} %copy-done.36), channel_id=1, replica_groups=mesh['dp'=8,'tensor'=4] {'dp'}, use_global_device_ids=true, to_apply=%region_26.27 | all-reduce | flops 1152 | bytes 9216 | tf_op jit(solution)/shard_map/psum | solution.py:213
  566.7 1.6 copy.48
  568.3 23.5 %reduce-scatter.25.cloned.1.call-done = f32[96,576]{1,0:T(8,128)} async-done(((f32[768,576]{1,0:T(8,128)}), f32[96,576]{1,0:T(8,128)}) %reduce-scatter.25.cloned.1.call-update) | async-done | bytes 221200
  593.7 37.6 %reduce-scatter.19.cloned.1.call-done = bf16[512,768]{1,0:T(8,128)(2,1)} async-done(((bf16[2048,768]{1,0:T(8,128)(2,1)}), bf16[512,768]{1,0:T(8,128)(2,1)}) %reduce-scatter.19.cloned.1.call-update) | async-done | bytes 786448 | tf_op jit(solution)/shard_map/reduce_scatter | solution.py:198
  631.3 1.8 convert_reduce_fusion.1
  633.1 2.1 fusion.40
  635.2 2.8 convert_reduce_fusion.4
  638.0 40.7 %all-reduce = (f32[768]{0:T(1024)}, f32[768]{0:T(1024)}, f32[768]{0:T(1024)}, f32[768]{0:T(1024)}, f32[768]{0:T(1024)}, /*index=5*/f32[768]{0:T(1024)}) all-reduce(f32[768]{0:T(1024)S(1)} %get-tuple-element.448, f32[768]{0:T(1024)S(1)} %get-tuple-element.451, ...), channel_id=1, replica_groups=mesh['dp'=8,'tensor'=4] {'dp','tensor'}, use_global_device_ids=true, to_apply=%region_20.21 | all-reduce | flops 4608 | bytes 36864 | tf_op jit(solution)/shard_map/psum | solution.py:209
  678.7 26.0 %reduce-scatter.23.cloned.1.call-done = f32[768,96]{0,1:T(8,128)} async-done(((f32[768,768]{0,1:T(8,128)}), f32[768,96]{0,1:T(8,128)}) %reduce-scatter.23.cloned.1.call-update) | async-done | bytes 294928 | tf_op jit(solution)/shard_map/reduce_scatter | solution.py:207
  704.6 72.1 %reduce-scatter.21.cloned.1.call-done = f32[96,768]{1,0:T(8,128)} async-done(((f32[768,768]{1,0:T(8,128)}), f32[96,768]{1,0:T(8,128)}) %reduce-scatter.21.cloned.1.call-update) | async-done | bytes 294928 | tf_op jit(solution)/shard_map/reduce_scatter | solution.py:206
  (258 shorter events, 79.4 us)
Async XLA Ops:
  8.0 5.4 copy-start.25
  8.0 5.6 copy-start.20
  8.0 76.7 %all-gather.7.cloned.1.call-start = ((), (), s32[]{:S(2)}) async-start(), calls=%async_computation.8 | async-start | bytes 3932160 | tf_op jit(solution)/shard_map/all_gather | solution.py:51
  9.4 4.1 copy-start.22
  10.9 2.6 copy-start.30
  11.0 2.6 copy-start.27
  13.4 71.4 %copy-start.37 = (f32[2,192]{1,0:T(2,128)S(1)}, f32[2,192]{1,0:T(2,128)}, u32[]{:S(2)}) copy-start(f32[2,192]{1,0:T(2,128)} %param.24) | copy-start | bytes 4612
  13.4 159.2 %reduce-scatter.13.cloned.1.call-start = ((), (), s32[]{:S(2)}) async-start(), calls=%async_computation.9 | async-start | bytes 3932160 | tf_op jit(solution)/shard_map/reduce_scatter | solution.py:99
  53.5 35.2 %copy-start.13 = (bf16[3,768,192]{1,2,0:T(8,128)(2,1)}, bf16[3,768,192]{1,2,0:T(8,128)(2,1)S(1)}, u32[]{:S(2)}) copy-start(bf16[3,768,192]{1,2,0:T(8,128)(2,1)S(1)} %copy.39) | copy-start | bytes 2654212
  88.7 0.7 copy-start.19
  129.7 5.4 copy-start.3
  129.7 5.4 copy-start.7
  131.5 0.9 copy-start.11
  132.4 40.2 %copy-start = (bf16[512,768]{1,0:T(8,128)(2,1)S(1)}, bf16[512,768]{1,0:T(8,128)(2,1)}, u32[]{:S(2)}) copy-start(bf16[512,768]{1,0:T(8,128)(2,1)} %param.19) | copy-start | bytes 2359300
  132.4 40.2 %copy-start.21 = (f32[768]{0:T(1024)S(1)}, f32[768]{0:T(1024)}, u32[]{:S(2)}) copy-start(f32[768]{0:T(1024)} %param.26) | copy-start | bytes 9220
  135.1 54.5 %all-gather.11.cloned.1.call-start = ((), (), s32[]{:S(2)}) async-start(), calls=%async_computation.11 | async-start | bytes 1327104 | tf_op jit(solution)/shard_map/all_gather | solution.py:46
  135.7 72.2 %all-gather.9.cloned.1.call-start = ((), (), s32[]{:S(2)}) async-start(), calls=%async_computation.10 | async-start | bytes 3932160 | tf_op jit(solution)/shard_map/all_gather | solution.py:104
  172.6 3.2 copy-start.4
  175.8 39.6 %copy-start.32 = (f32[512]{0:T(512)}, f32[512]{0:T(512)S(1)}, u32[]{:S(2)}) copy-start(f32[512]{0:T(512)S(1)} %multiply_reduce_fusion.1) | copy-start | bytes 6148
  175.8 168.9 %copy-start.29 = (f32[512]{0:T(512)}, f32[512]{0:T(512)S(1)}, u32[]{:S(2)}) copy-start(f32[512]{0:T(512)S(1)} %fusion.55) | copy-start | bytes 6148
  177.9 73.9 %all-gather.13.cloned.1.call-start = ((), (), s32[]{:S(2)}) async-start(), calls=%async_computation.12 | async-start | bytes 1327104 | tf_op jit(solution)/shard_map/all_gather | solution.py:47
  178.4 101.9 %all-gather.15.cloned.1.call-start = ((), (), s32[]{:S(2)}) async-start(), calls=%async_computation.14 | async-start | bytes 3932160 | tf_op jit(solution)/shard_map/all_gather | solution.py:115
  179.2 101.1 %copy-start.35 = (f32[768]{0:T(1024)S(1)}, f32[768]{0:T(1024)}, u32[]{:S(2)}) copy-start(f32[768]{0:T(1024)} %param.30) | copy-start | bytes 9220
  179.2 165.5 %reduce-scatter.17.cloned.1.call-start = ((), (), s32[]{:S(2)}) async-start(), calls=%async_computation.15 | async-start | bytes 3932160 | tf_op jit(solution)/shard_map/reduce_scatter | solution.py:128
  280.3 22.3 %copy-start.39 = (bf16[768,768]{1,0:T(8,128)(2,1)S(1)}, bf16[768,768]{1,0:T(8,128)(2,1)}, u32[]{:S(2)}) copy-start(bf16[768,768]{1,0:T(8,128)(2,1)} %all-gather.11.cloned.1.call-done) | copy-start | bytes 3538948
  300.9 1.7 copy-start.41
  306.6 78.5 %reduce-scatter.15.cloned.1.call-start = ((), (), s32[]{:S(2)}) async-start(), calls=%async_computation.13 | async-start | bytes 3932160 | tf_op jit(solution)/shard_map/reduce_scatter | solution.py:109
  306.7 7.2 copy-start.40
  312.3 1.6 copy-start.10
  317.9 26.8 %copy-start.26 = (f32[768]{0:T(1024)S(1)}, f32[768]{0:T(1024)}, u32[]{:S(2)}) copy-start(f32[768]{0:T(1024)} %param.27) | copy-start | bytes 9220
  318.0 101.3 %all-gather.17.cloned.1.call-start = ((), (), s32[]{:S(2)}) async-start(), calls=%async_computation.16 | async-start | bytes 3932160 | tf_op jit(solution)/shard_map/all_gather | solution.py:135
  347.3 42.3 %copy-start.9 = (bf16[512,768]{1,0:T(8,128)(2,1)S(1)}, bf16[512,768]{1,0:T(8,128)(2,1)}, u32[]{:S(2)}) copy-start(bf16[512,768]{1,0:T(8,128)(2,1)} %param.33) | copy-start | bytes 2359300
  388.3 1.2 copy-start.5
  388.3 31.0 %copy-start.12 = (bf16[4,24,8,512]{3,2,0,1:T(8,128)(2,1)S(1)}, bf16[4,24,8,512]{3,2,0,1:T(8,128)(2,1)}, u32[]{:S(2)}) copy-start(bf16[4,24,8,512]{3,2,0,1:T(8,128)(2,1)} %copy-done.11) | copy-start | bytes 2359300
  390.8 175.9 %reduce-scatter.27.cloned.1.call-start = ((), (), s32[]{:S(2)}) async-start(), calls=%async_computation.21 | async-start | bytes 884736
  423.4 168.3 %reduce-scatter.25.cloned.1.call-start = ((), (), s32[]{:S(2)}) async-start(), calls=%async_computation.20 | async-start | bytes 2211840
  446.1 1.4 copy-start.1
  447.9 1.1 copy-start.2
  465.8 1.4 copy-start.1
  467.6 1.1 copy-start.2
  485.5 1.4 copy-start.1
  487.3 1.1 copy-start.2
  505.2 1.4 copy-start.1
  507.0 1.1 copy-start.2
  511.6 2.9 copy-start.15
  511.6 2.9 copy-start.38
  513.4 0.9 copy-start.16
  513.5 1.0 copy-start.18
  519.3 5.0 copy-start.14
  519.3 5.0 copy-start.17
  524.2 107.0 %reduce-scatter.19.cloned.1.call-start = ((), (), s32[]{:S(2)}) async-start(), calls=%async_computation.17 | async-start | bytes 3932160 | tf_op jit(solution)/shard_map/reduce_scatter | solution.py:198
  529.8 174.9 %reduce-scatter.23.cloned.1.call-start = ((), (), s32[]{:S(2)}) async-start(), calls=%async_computation.19 | async-start | bytes 2654208 | tf_op jit(solution)/shard_map/reduce_scatter | solution.py:207
  537.0 7.1 copy-start.36
  537.0 239.7 %reduce-scatter.21.cloned.1.call-start = ((), (), s32[]{:S(2)}) async-start(), calls=%async_computation.18 | async-start | bytes 2654208 | tf_op jit(solution)/shard_map/reduce_scatter | solution.py:206
  544.0 87.2 %copy-start.23 = (f32[512]{0:T(512)S(1)}, f32[512]{0:T(512)}, u32[]{:S(2)}) copy-start(f32[512]{0:T(512)} %copy-done.22) | copy-start | bytes 6148
  544.0 87.2 %copy-start.24 = (f32[768]{0:T(1024)S(1)}, f32[768]{0:T(1024)}, u32[]{:S(2)}) copy-start(f32[768]{0:T(1024)} %param.21) | copy-start | bytes 9220
  544.0 89.0 %copy-start.31 = (f32[512]{0:T(512)S(1)}, f32[512]{0:T(512)}, u32[]{:S(2)}) copy-start(f32[512]{0:T(512)} %copy-done.30) | copy-start | bytes 6148
  544.0 89.0 %copy-start.28 = (f32[512]{0:T(512)S(1)}, f32[512]{0:T(512)}, u32[]{:S(2)}) copy-start(f32[512]{0:T(512)} %copy-done.27) | copy-start | bytes 6148
  544.0 91.1 %copy-start.6 = (f32[512,768]{1,0:T(8,128)S(1)}, f32[512,768]{1,0:T(8,128)}, u32[]{:S(2)}) copy-start(f32[512,768]{1,0:T(8,128)} %copy-done.5) | copy-start | bytes 4718596
  631.3 3.9 copy-start.8
  633.0 5.0 copy-start.33
  633.1 5.0 copy-start.34
Sparse Core Ops, SparseCore 0:
  13.5 31.2 all-gather.6
  135.2 37.3 reduce-scatter.12
  306.7 37.9 reduce-scatter.16
  347.1 37.9 reduce-scatter.14
Sparse Core Ops, SparseCore 1:
  138.0 40.8 all-gather.10
  181.0 26.8 all-gather.8
  210.2 41.5 all-gather.12
  253.4 26.8 all-gather.14
  390.9 28.4 all-gather.16
  423.5 62.6 reduce-scatter.26
  524.3 67.4 reduce-scatter.24
  594.3 36.9 reduce-scatter.18
  635.2 69.4 reduce-scatter.22
  708.7 67.9 reduce-scatter.20
where the time goes:
time: 793 us; the launch traced here: 784 us
  waiting for transfers between devices  373 us (47%)
  blocking collectives  133 us (17%)
  matrix products  113 us (14%)
  other arithmetic  55.6 us (7%)
  local copies, waits for them, and re-layouts  55.3 us (7%)
  loops' own time  27.1 us (3%)
  between operations  16 us (2%)
  starting transfers between devices  10.9 us (1%)
    reduce_scatter x1, waiting for transfers between devices, body(): lax.psum_scatter(grad_w_up_full, 'dp', scatter_dimension=0, tiled=True)  72.1 us
    psum x1, blocking collectives, body(): lax.psum((grad_gain1, grad_bias1, grad_out_local, grad_gain2, grad_bias2,...  40.7 us
    all_gather x1, blocking collectives, body(): lax.all_gather(w_qkv, 'dp', axis=1, tiled=True)  38.9 us
    reduce_scatter x1, waiting for transfers between devices, body(): lax.psum_scatter(partial_norm1.astype(jnp.bfloat16), 'tensor', scatter_di...  37.6 us
    reduce_scatter x1, waiting for transfers between devices, body(): lax.psum_scatter(partial_attn.astype(jnp.bfloat16), 'tensor', scatter_dim...  36.8 us
    reduce_scatter x1, waiting for transfers between devices, body(): lax.psum_scatter(partial_mlp.astype(jnp.bfloat16), 'tensor', scatter_dime...  36.5 us
    all_gather x1, waiting for transfers between devices, body(): lax.all_gather(w_down, 'dp', axis=1, tiled=True)  36.4 us
    all_gather x1, blocking collectives, body(): lax.all_gather(w_out, 'dp', axis=1, tiled=True)  31.2 us
  transfers between devices with their start and end apart: 14, of which 11 were waited for; matrix products, arithmetic and copies ran while one was open for 17% of the time, Pallas kernels for 0%

commit v1 on v0

v1 whole, which is shorter than its diff:
```python
from functools import partial

import jax
import jax.numpy as jnp
from jax import lax
from jax.experimental import pallas as pl
from jax.experimental.pallas import tpu as pltpu
from jax.sharding import PartitionSpec as P

HEAD_DIM = 64
BLOCK = 256
LOW = jnp.bfloat16
WIDE = jnp.float32
BLOCKED = -1e30


def dot(a, b):
    return jnp.dot(a, b, preferred_element_type=WIDE)


def dot_last(a, b):
    return lax.dot_general(a, b, (((1,), (1,)), ((), ())), preferred_element_type=WIDE)


def dot_first(a, b):
    return lax.dot_general(a, b, (((0,), (0,)), ((), ())), preferred_element_type=WIDE)


def params(megabytes=40):
    return pltpu.CompilerParams(vmem_limit_bytes=megabytes * 1024 * 1024)


def cost(flops, moved, exps=0):
    return pl.CostEstimate(flops=int(flops), bytes_accessed=int(moved), transcendentals=int(exps))


def centered(values):
    center = values - jnp.mean(values, -1, keepdims=True)
    spread = jnp.mean(center * center, -1, keepdims=True)
    return center, lax.rsqrt(spread + 1e-05)


def project_kernel(x_ref, gain_ref, bias_ref, w0_ref, w1_ref, shift_ref, scale_ref, n_ref, p0_ref, p1_ref):
    center, inverse = centered(x_ref[...].astype(WIDE))
    normed = (center * inverse * gain_ref[...] + bias_ref[...]).astype(LOW)
    n_ref[...] = normed
    width = p0_ref.shape[1]
    for number, (w_ref, p_ref) in enumerate(((w0_ref, p0_ref), (w1_ref, p1_ref))):
        proj = dot(normed, w_ref[:, :width])
        p_ref[...] = ((proj + shift_ref[number : number + 1]) * scale_ref[...]).astype(LOW)


def project(both, gain, bias, w0, w1, shift, scale):
    tokens, d = both.shape[0], w0.shape[0]
    width = shift.shape[1]
    whole = lambda a: pl.BlockSpec(a.shape, lambda i: (0, 0))
    rows = lambda n: pl.BlockSpec((BLOCK, n), lambda i: (i, 0))
    return pl.pallas_call(
        project_kernel,
        grid=(tokens // BLOCK,),
        in_specs=[rows(d)] + [whole(a) for a in (gain, bias, w0, w1, shift, scale)],
        out_specs=[rows(d), rows(width), rows(width)],
        out_shape=[
            jax.ShapeDtypeStruct((tokens, d), LOW),
            jax.ShapeDtypeStruct((tokens, width), LOW),
            jax.ShapeDtypeStruct((tokens, width), LOW),
        ],
        compiler_params=params(),
        cost_estimate=cost(4 * tokens * d * width, 8 * tokens * d),
        name="project",
    )(both, gain, bias, w0, w1, shift, scale)


def features(seg, heads_values, blocked):
    lane = lax.broadcasted_iota(jnp.int32, (seg.shape[0], HEAD_DIM), 1)
    same = lane == seg
    if blocked:
        extra = jnp.where(same | (lane > 3), 0.0, BLOCKED)
    else:
        extra = jnp.where(same, 1.0, 0.0)
    return jnp.concatenate([heads_values, extra.astype(LOW)], axis=1)


def causal(scores_t):
    key = lax.broadcasted_iota(jnp.int32, scores_t.shape, 0)
    query = lax.broadcasted_iota(jnp.int32, scores_t.shape, 1)
    return jnp.where(key <= query, scores_t, BLOCKED)


def attend_kernel(p_ref, seg_ref, out_ref, log_ref):
    length = p_ref.shape[0]
    heads = p_ref.shape[1] // (3 * HEAD_DIM)
    seg = seg_ref[...]
    logs = []
    outs = [jnp.zeros((length, HEAD_DIM), LOW)]
    for head in range(heads):
        at = lambda c: slice((c * heads + head) * HEAD_DIM, (c * heads + head + 1) * HEAD_DIM)
        query = features(seg, p_ref[:, at(0)], True)
        key = features(seg, p_ref[:, at(1)], False)
        value = p_ref[:, at(2)]
        head_logs, head_outs = [], []
        for block in range(length // BLOCK):
            start, stop = block * BLOCK, (block + 1) * BLOCK
            scores = dot_last(key[:stop], query[start:stop])
            last = causal(scores[start:])
            scores = last if block == 0 else jnp.concatenate([scores[:start], last], axis=0)
            top = jnp.max(scores, 0, keepdims=True)
            shifted = jnp.exp(scores - top)
            total = jnp.sum(shifted, 0, keepdims=True)
            result = dot_first(value[:stop], shifted.astype(LOW)) / total
            head_logs.append(top + jnp.log(total))
            head_outs.append(result.T.astype(LOW))
        logs.append(jnp.concatenate(head_logs, axis=1))
        outs.append(jnp.concatenate(head_outs, axis=0))
    out_ref[...] = jnp.concatenate(outs, axis=1)
    logs.append(jnp.zeros((8 - heads, length), WIDE))
    log_ref[...] = jnp.concatenate(logs, axis=0)


def attend(proj, seg):
    length, width = proj.shape
    heads = width // (3 * HEAD_DIM)
    return pl.pallas_call(
        attend_kernel,
        out_shape=[
            jax.ShapeDtypeStruct((length, (heads + 1) * HEAD_DIM), LOW),
            jax.ShapeDtypeStruct((8, length), WIDE),
        ],
        compiler_params=params(),
        cost_estimate=cost(heads * 4 * length * length * HEAD_DIM, 4 * length * width, heads * length * length),
        name="attend",
    )(proj, seg)


def attend_back_kernel(p_ref, seg_ref, out_ref, log_ref, grad_ref, gp_ref, sum_ref, dq_ref):
    length = p_ref.shape[0]
    heads = p_ref.shape[1] // (3 * HEAD_DIM)
    seg = seg_ref[...]
    pieces = [[], [], []]
    for head in range(heads):
        at = lambda c: slice((c * heads + head) * HEAD_DIM, (c * heads + head + 1) * HEAD_DIM)
        shifted_at = slice((head + 1) * HEAD_DIM, (head + 2) * HEAD_DIM)
        plain = p_ref[:, at(0)]
        query = features(seg, plain, True)
        plain_key = p_ref[:, at(1)]
        key = features(seg, plain_key, False)
        value = p_ref[:, at(2)]
        grad = grad_ref[:, shifted_at]
        log_row = log_ref[head : head + 1]
        product = grad.astype(WIDE) * out_ref[:, shifted_at].astype(WIDE)
        inner = jnp.sum(product.T, 0, keepdims=True)
        dks, dvs = [], []
        for block in range(length // BLOCK):
            start, stop = block * BLOCK, (block + 1) * BLOCK
            scores = dot_last(key[start:stop], query[start:])
            first = causal(scores[:, :BLOCK])
            if stop < length:
                first = jnp.concatenate([first, scores[:, BLOCK:]], axis=1)
            probs = jnp.exp(first - log_row[:, start:])
            grad_probs = dot_last(value[start:stop], grad[start:])
            grad_scores = (probs * (grad_probs - inner[:, start:])).astype(LOW)
            dvs.append(dot(probs.astype(LOW), grad[start:]).astype(LOW))
            dks.append(dot(grad_scores, plain[start:]).astype(LOW))
            part = dot_first(plain_key[start:stop], grad_scores)
            if block == 0:
                dq_ref[...] = part
            else:
                dq_ref[:, start:] += part
        dq = (dq_ref[...].T.astype(LOW).astype(WIDE) * HEAD_DIM ** (-0.5)).astype(LOW)
        pieces[0].append(dq)
        pieces[1].append(jnp.concatenate(dks, axis=0))
        pieces[2].append(jnp.concatenate(dvs, axis=0))
    grads = jnp.concatenate(pieces[0] + pieces[1] + pieces[2], axis=1)
    gp_ref[...] = grads
    sum_ref[...] = jnp.sum(grads.astype(WIDE), 0, keepdims=True)


def attend_back(proj, seg, out, logs, grad):
    length, width = proj.shape
    heads = width // (3 * HEAD_DIM)
    return pl.pallas_call(
        attend_back_kernel,
        out_shape=[
            jax.ShapeDtypeStruct((length, width), LOW),
            jax.ShapeDtypeStruct((1, width), WIDE),
        ],
        scratch_shapes=[pltpu.VMEM((HEAD_DIM, length), WIDE)],
        compiler_params=params(),
        cost_estimate=cost(heads * 10 * length * length * HEAD_DIM, 8 * length * width, heads * length * length),
        name="attend_back",
    )(proj, seg, out, logs, grad)


def mlp_kernel(
    x_ref, cot_ref, pa_ref, pb_ref, ob_ref, gain_ref, bias_ref, ub_ref, up0_ref, up1_ref, dn0_ref, dn1_ref,
    mid_ref, n_ref, act_ref, gu_ref, mlp_ref, gn_ref, sum_ref,
):
    middle = x_ref[...].astype(WIDE) + (pa_ref[...].astype(WIDE) + pb_ref[...].astype(WIDE)) + ob_ref[...]
    mid_ref[...] = middle
    center, inverse = centered(middle)
    normed = (center * inverse * gain_ref[...] + bias_ref[...]).astype(LOW)
    n_ref[...] = normed
    cot = cot_ref[...]
    width = up0_ref.shape[1]
    chunk = width // 2

    @pl.when(pl.program_id(0) == 0)
    def _():
        sum_ref[...] = jnp.zeros_like(sum_ref)

    mlp = grad_normed = None
    for number, (up_ref, dn_ref) in enumerate(((up0_ref, dn0_ref), (up1_ref, dn1_ref))):
        for start in range(0, width, chunk):
            at = slice(start, start + chunk)
            to = slice(number * width + start, number * width + start + chunk)
            upper = dot(normed, up_ref[:, at]) + ub_ref[number : number + 1, at]
            grad_active = dot(cot, dn_ref[:, at])
            phi = 0.5 + 0.5 * lax.erf(upper * 0.5**0.5)
            density = jnp.exp(-0.5 * (upper * upper)) * 0.3989422804014327
            active = (upper * phi).astype(LOW)
            grad_upper = (grad_active * (phi + upper * density)).astype(LOW)
            act_ref[:, to] = active
            gu_ref[:, to] = grad_upper
            sum_ref[:, to] += jnp.sum(grad_upper.astype(WIDE), 0, keepdims=True)
            a = dot_last(active, dn_ref[:, at])
            b = dot_last(grad_upper, up_ref[:, at])
            mlp = a if mlp is None else mlp + a
            grad_normed = b if grad_normed is None else grad_normed + b
    mlp_ref[...] = mlp.astype(LOW)
    gn_ref[...] = grad_normed.astype(LOW)


def mlp_pass(both, pa, pb, out_bias, gain, bias, up_bias, up0, up1, dn0, dn1):
    tokens, d = pa.shape
    width = up0.shape[1]
    whole = lambda a: pl.BlockSpec(a.shape, lambda i: (0, 0))
    rows = lambda n: pl.BlockSpec((BLOCK, n), lambda i: (i, 0))
    shape = jax.ShapeDtypeStruct
    return pl.pallas_call(
        mlp_kernel,
        grid=(tokens // BLOCK,),
        in_specs=[rows(d), pl.BlockSpec((BLOCK, d), lambda i: (i, 1)), rows(d), rows(d)]
        + [whole(a) for a in (out_bias, gain, bias, up_bias, up0, up1, dn0, dn1)],
        out_specs=[rows(d), rows(d), rows(2 * width), rows(2 * width), rows(d), rows(d)]
        + [pl.BlockSpec((1, 2 * width), lambda i: (0, 0))],
        out_shape=[
            shape((tokens, d), WIDE),
            shape((tokens, d), LOW),
            shape((tokens, 2 * width), LOW),
            shape((tokens, 2 * width), LOW),
            shape((tokens, d), LOW),
            shape((tokens, d), LOW),
            shape((1, 2 * width), WIDE),
        ],
        compiler_params=params(),
        cost_estimate=cost(16 * tokens * d * width, 30 * tokens * d, 4 * tokens * width),
        name="mlp_pass",
    )(both, both, pa, pb, out_bias, gain, bias, up_bias, up0, up1, dn0, dn1)


def norm_back_kernel(mid_ref, cot_ref, ga_ref, gb_ref, gain_ref, w0_ref, w1_ref, gm_ref, low_ref, g0_ref, g1_ref, sum_ref):
    e = ga_ref[...].astype(WIDE) + gb_ref[...].astype(WIDE)
    cot = cot_ref[...].astype(WIDE)
    center, inverse = centered(mid_ref[...])
    normal = center * inverse
    f = e * gain_ref[...]
    grad = inverse * (f - jnp.mean(f, -1, keepdims=True) - normal * jnp.mean(f * normal, -1, keepdims=True))
    grad_mid = cot + grad
    gm_ref[...] = grad_mid
    low = grad_mid.astype(LOW)
    low_ref[...] = low
    split = w0_ref.shape[1] - g0_ref.shape[1]
    g0_ref[...] = dot(low, w0_ref[:, split:]).astype(LOW)
    g1_ref[...] = dot(low, w1_ref[:, split:]).astype(LOW)

    @pl.when(pl.program_id(0) == 0)
    def _():
        sum_ref[...] = jnp.zeros_like(sum_ref)

    for row, term in enumerate((e * normal, e, low.astype(WIDE), cot)):
        sum_ref[row : row + 1] += jnp.sum(term, 0, keepdims=True)


def norm_back(mid, both, ga, gb, gain, w0, w1, width):
    tokens, d = mid.shape
    whole = lambda a: pl.BlockSpec(a.shape, lambda i: (0, 0))
    rows = lambda n: pl.BlockSpec((BLOCK, n), lambda i: (i, 0))
    shape = jax.ShapeDtypeStruct
    return pl.pallas_call(
        norm_back_kernel,
        grid=(tokens // BLOCK,),
        in_specs=[rows(d), pl.BlockSpec((BLOCK, d), lambda i: (i, 1)), rows(d), rows(d)]
        + [whole(a) for a in (gain, w0, w1)],
        out_specs=[rows(d), rows(d), rows(width), rows(width), pl.BlockSpec((8, d), lambda i: (0, 0))],
        out_shape=[
            shape((tokens, d), WIDE),
            shape((tokens, d), LOW),
            shape((tokens, width), LOW),
            shape((tokens, width), LOW),
            shape((8, d), WIDE),
        ],
        compiler_params=params(),
        cost_estimate=cost(4 * tokens * d * width, 20 * tokens * d),
        name="norm_back",
    )(mid, both, ga, gb, gain, w0, w1)


def swap(value, axis, bit):
    size = lax.axis_size(axis)
    return lax.ppermute(value, axis, [(i, i ^ bit) for i in range(size)])


def has(axis, bit):
    return (lax.axis_index(axis) // bit) % 2 == 1


def in_order(flag, own, other, axis):
    return jnp.concatenate([jnp.where(flag, other, own), jnp.where(flag, own, other)], axis=axis)


def far_bits(size):
    bit, bits = size // 2, []
    while bit > 1:
        bits.append(bit)
        bit //= 2
    return bits


def spread_far(piece):
    held = piece[None]
    for level, bit in enumerate(far_bits(lax.axis_size("dp"))):
        held = in_order(has("dp", bit), held[:, None], swap(held, "dp", bit)[:, None], 1)
        held = held.reshape((2 ** (level + 1),) + piece.shape)
    return held


def rows_of(parts, mine):
    ordered = in_order(has("dp", 1), parts[:, None], mine[:, None], 1)
    return ordered.reshape(-1, parts.shape[-1])


def spread_x_first(held):
    own = rows_of(held, swap(held, "dp", 1))
    return own, swap(own, "tensor", 2)


def spread_y_first(held):
    pair = jnp.stack([held, swap(held, "tensor", 2)])
    there = swap(pair, "dp", 1)
    return rows_of(pair[0], there[0]), rows_of(pair[1], there[1])


def halves(grad):
    size = lax.axis_size("dp")
    parts = grad.reshape(size // 2, 2, grad.shape[0] // size, grad.shape[1])
    flag = has("dp", 1)
    return jnp.where(flag, parts[:, 1], parts[:, 0]), jnp.where(flag, parts[:, 0], parts[:, 1])


def added(a, b):
    return (a.astype(WIDE) + b.astype(WIDE)).astype(LOW)


def collect_y_first(own, other):
    kept, sent = halves(added(own, swap(other, "tensor", 2)))
    return added(kept, swap(sent, "dp", 1))


def collect_x_first(own, other):
    kept_own, sent_own = halves(own)
    kept_other, sent_other = halves(other)
    there = swap(jnp.stack([sent_own, sent_other]), "dp", 1)
    return added(added(kept_own, there[0]), swap(added(kept_other, there[1]), "tensor", 2))


def collect_far(held):
    for bit in reversed(far_bits(lax.axis_size("dp"))):
        pairs = held.reshape((held.shape[0] // 2, 2) + held.shape[1:])
        flag = has("dp", bit)
        kept = jnp.where(flag, pairs[:, 1], pairs[:, 0])
        sent = jnp.where(flag, pairs[:, 0], pairs[:, 1])
        held = kept.astype(WIDE) + swap(sent, "dp", bit).astype(WIDE)
        if held.shape[0] > 1:
            held = held.astype(LOW)
    return held[0].astype(WIDE)


def body(
    hidden, segment_ids, norm1_gain, norm1_bias, w_qkv, qv_bias, w_out, out_bias,
    norm2_gain, norm2_bias, w_up, up_bias, w_down, down_bias, cotangent,
):
    mine, d = hidden.shape
    shard, width = w_qkv.shape[1], w_qkv.shape[2]
    core = has("tensor", 1)
    row = lambda v: v.reshape(1, -1)

    first = jnp.concatenate([w_qkv[0], w_qkv[1], w_qkv[2], w_out.T], axis=1)
    second = jnp.concatenate([w_up, w_down.T], axis=1)
    far_first = spread_far(first)
    a0, a1 = spread_x_first(far_first[..., : 2 * width])
    b0, b1 = spread_y_first(far_first[..., 2 * width :])
    w0, w1 = jnp.concatenate([a0, b0], axis=1), jnp.concatenate([a1, b1], axis=1)
    far_second = spread_far(second)
    up0, up1 = spread_x_first(far_second[..., : w_up.shape[1]])
    dn0, dn1 = spread_y_first(far_second[..., w_up.shape[1] :])
    biases = jnp.concatenate([qv_bias.reshape(-1), up_bias])
    other_biases = swap(biases, "tensor", 2)
    ub = jnp.stack([up_bias, other_biases[2 * width :]])
    none = jnp.zeros((width,), WIDE)
    shift = jnp.stack(
        [jnp.concatenate([v[:width], none, v[width : 2 * width]]) for v in (biases, other_biases)]
    )
    scale = jnp.concatenate([none + HEAD_DIM ** (-0.5), none + 1.0, none + 1.0]).reshape(1, -1)

    pair = jnp.concatenate([hidden, cotangent], axis=1)
    both = in_order(core, pair, swap(pair, "tensor", 1), 0)
    seg = lax.dynamic_index_in_dim(segment_ids, lax.axis_index("tensor") // 2, 0, keepdims=False)
    seg = seg.reshape(-1, 1)
    here = lax.axis_index("tensor") % 2 * mine
    there = mine - here

    n1, p0, p1 = project(both, row(norm1_gain), row(norm1_bias), w0, w1, shift, scale)
    att0, log0 = attend(p0, seg)
    att1, log1 = attend(p1, seg)
    cut = w0.shape[1] - att0.shape[1]
    pa = (dot_last(att0, w0[:, cut:]) + dot_last(att1, w1[:, cut:])).astype(LOW)
    pb = swap(pa, "tensor", 1)
    middle, n2, active, grad_upper, mlp, ga, up_sums = mlp_pass(
        both, pa, pb, row(out_bias), row(norm2_gain), row(norm2_bias), ub, up0, up1, dn0, dn1
    )
    mlp_there = swap(lax.dynamic_slice_in_dim(mlp, there, mine, 0), "tensor", 1)
    mlp_here = lax.dynamic_slice_in_dim(mlp, here, mine, 0)
    output = lax.dynamic_slice_in_dim(middle, here, mine, 0) + down_bias
    output = (output + (mlp_here.astype(WIDE) + mlp_there.astype(WIDE))).astype(LOW)

    gb = swap(ga, "tensor", 1)
    cot_all = both[:, d:]
    half = w_up.shape[1]
    low_dot = lambda a, b: dot_first(a, b).astype(LOW)
    grad_mid, grad_attn, gatt0, gatt1, sums = norm_back(
        middle, both, ga, gb, row(norm2_gain), w0, w1, att0.shape[1]
    )
    down = collect_y_first(low_dot(cot_all, active[:, :half]), low_dot(cot_all, active[:, half:]))
    up = collect_x_first(low_dot(n2, grad_upper[:, :half]), low_dot(n2, grad_upper[:, half:]))
    second_grad = collect_far(jnp.concatenate([up, down], axis=2))

    gp0, gsum0 = attend_back(p0, seg, att0, log0, gatt0)
    gp1, gsum1 = attend_back(p1, seg, att1, log1, gatt1)

    def branch(start):
        cut_rows = lambda v: lax.dynamic_slice_in_dim(v, start, mine, 0)
        return dot_last(cut_rows(gp0), w0[:, : 3 * width]) + dot_last(cut_rows(gp1), w1[:, : 3 * width])

    from_there = swap(branch(there).astype(LOW), "tensor", 1)
    grad_normed1 = branch(here) + from_there.astype(WIDE)

    tail0, tail1 = [
        jnp.concatenate([low_dot(n1, gp[:, 2 * width :]), low_dot(grad_attn, att[:, HEAD_DIM:])], axis=1)
        for gp, att in ((gp0, att0), (gp1, att1))
    ]
    front = collect_x_first(low_dot(n1, gp0[:, : 2 * width]), low_dot(n1, gp1[:, : 2 * width]))
    tail = collect_y_first(tail0, tail1)
    first_grad = collect_far(jnp.concatenate([front, tail], axis=2))

    center, inverse = centered(hidden.astype(WIDE))
    normal = center * inverse
    f = grad_normed1 * norm1_gain
    grad_input = inverse * (f - jnp.mean(f, -1, keepdims=True) - normal * jnp.mean(f * normal, -1, keepdims=True))
    grad_hidden = (lax.dynamic_slice_in_dim(grad_mid, here, mine, 0) + grad_input).astype(LOW)

    norm1_sums = jnp.stack([jnp.sum(grad_normed1 * normal, 0), jnp.sum(grad_normed1, 0)])
    norm1_sums = norm1_sums + swap(norm1_sums, "tensor", 1)
    shared = jnp.concatenate([norm1_sums.reshape(-1), sums[:4].reshape(-1)])
    part = lambda gsum, at: jnp.concatenate(
        [gsum[0, :width], gsum[0, 2 * width :], up_sums[0, at : at + half]]
    )
    sent = swap(jnp.concatenate([shared, part(gsum1, half)]), "tensor", 2)
    total = jnp.concatenate([shared, part(gsum0, 0)]) + sent
    bit = 1
    while bit < lax.axis_size("dp"):
        total = total + swap(total, "dp", bit)
        bit *= 2
    norm1_gain_grad, norm1_bias_grad, gain2, bias2, out_grad, down_grad = (
        total[i * d : (i + 1) * d] for i in range(6)
    )
    own = total[6 * d :]
    columns = lambda i: first_grad[:, i * width : (i + 1) * width]
    return (
        output,
        grad_hidden,
        norm1_gain_grad,
        norm1_bias_grad,
        jnp.stack([columns(0), columns(1), columns(2)]),
        own[: 2 * width].reshape(2, width),
        columns(3).T,
        out_grad,
        gain2,
        bias2,
        second_grad[:, :half],
        own[2 * width :],
        second_grad[:, half:].T,
        down_grad,
    )


def solution(mesh):
    placed = (
        P(("dp", "tensor"), None),
        P("dp", None),
        P(),
        P(),
        P(None, "dp", "tensor"),
        P(None, "tensor"),
        P("tensor", "dp"),
        P(),
        P(),
        P(),
        P("dp", "tensor"),
        P("tensor"),
        P("tensor", "dp"),
        P(),
        P(("dp", "tensor"), None),
    )
    return jax.shard_map(
        body,
        mesh=mesh,
        in_specs=placed,
        out_specs=(
            P(("dp", "tensor"), None),
            P(("dp", "tensor"), None),
            P(),
            P(),
            P(None, "dp", "tensor"),
            P(None, "tensor"),
            P("tensor", "dp"),
            P(),
            P(),
            P(),
            P("dp", "tensor"),
            P("tensor"),
            P("tensor", "dp"),
            P(),
        ),
        check_vma=False,
    )
```

time: 793 us -> 297 us (0.37)
  waiting for transfers between devices: 373 us -> 106 us
  blocking collectives: 133 us -> 0 us
  matrix products: 113 us -> 21.2 us
  Pallas kernels: 0 us -> 52.9 us
  local copies, waits for them, and re-layouts: 55.3 us -> 20.6 us
  starting transfers between devices: 10.9 us -> 43.2 us
  loops' own time: 27.1 us -> 0 us
  between operations: 16 us -> 2.44 us
  other arithmetic: 55.6 us -> 45.5 us
    reduce_scatter x6 -> x0, waiting for transfers between devices: 236 us -> none  [the longest x1 72.1 us: body(): lax.psum_scatter(grad_w_up_full, 'dp', scatter_dimension=0, tiled=True)]
    all_gather x6 -> x0, waiting for transfers between devices: 112 us -> none  [the longest x1 36.4 us: body(): lax.all_gather(w_down, 'dp', axis=1, tiled=True)]
    ppermute x0 -> x35, waiting for transfers between devices: none -> 106 us  [swap(): return lax.ppermute(value, axis, [(i, i ^ bit) for i in range(size)])]
    dot_general x38 -> x16, matrix products: 105 us -> 21.2 us  [the longest x10 13.6 us: dot_first(): lax.dot_general(a, b, (((0,), (0,)), ((), ())), preferred_element_type=WIDE)]
    all_gather x2 -> x0, blocking collectives: 70.1 us -> none  [the longest x1 38.9 us: body(): lax.all_gather(w_qkv, 'dp', axis=1, tiled=True)]
    psum x2 -> x0, blocking collectives: 63.2 us -> none  [the longest x1 40.7 us: body(): lax.psum((grad_gain1, grad_bias1, grad_out_local, grad_gain2, grad_bias2,...]
    pallas_call x0 -> x7, Pallas kernels: none -> 52.9 us  [the longest x1 19.8 us: mlp_pass(): pl.pallas_call(mlp_kernel, grid=(tokens // BLOCK,), in_specs=[rows(d), pl...]
    ppermute x0 -> x35, starting transfers between devices: none -> 43.2 us  [swap(): return lax.ppermute(value, axis, [(i, i ^ bit) for i in range(size)])]
  transfers between devices with their start and end apart: 14 -> 35, of which waited for: 11 -> 17; matrix products, arithmetic and copies ran while one was open for 17% -> 24% of each run, Pallas kernels for 0% -> 11%
where the time goes in v1:
time: 297 us; the launch traced here: 292 us
  waiting for transfers between devices  106 us (36%)
  Pallas kernels  52.9 us (18%)
  other arithmetic  45.5 us (15%)
  starting transfers between devices  43.2 us (15%)
  matrix products  21.2 us (7%)
  local copies, waits for them, and re-layouts  20.6 us (7%)
    ppermute x35, waiting for transfers between devices, swap(): return lax.ppermute(value, axis, [(i, i ^ bit) for i in range(size)])  106 us
    ppermute x35, starting transfers between devices, swap(): return lax.ppermute(value, axis, [(i, i ^ bit) for i in range(size)])  43.2 us
    pallas_call x1, Pallas kernels, mlp_pass(): pl.pallas_call(mlp_kernel, grid=(tokens // BLOCK,), in_specs=[rows(d), pl...  19.8 us
    dot_general x10, matrix products, dot_first(): lax.dot_general(a, b, (((0,), (0,)), ((), ())), preferred_element_type=WIDE)  13.6 us
    pallas_call x2, Pallas kernels, attend_back(): pl.pallas_call(attend_back_kernel, out_shape=[jax.ShapeDtypeStruct((lengt...  11.5 us
    pallas_call x2, Pallas kernels, attend(): pl.pallas_call(attend_kernel, out_shape=[jax.ShapeDtypeStruct((length, (h...  10.8 us
    convert_element_type x8, other arithmetic, added(): return (a.astype(WIDE) + b.astype(WIDE)).astype(LOW)  10.5 us
    unnamed x141, local copies, waits for them, and re-layouts  10.1 us
  transfers between devices with their start and end apart: 35, of which 17 were waited for; matrix products, arithmetic and copies ran while one was open for 24% of the time, Pallas kernels for 11%

profile of v1, /device:TPU:0, one launch (start us, length us, event | category | flops | bytes accessed | tf_op | source)
XLA Modules:
  0.0 292.1 jit_solution(18154804354293027350)
XLA Ops:
  0.7 1.8 maximum_bitcast_fusion.2
  2.5 4.0 %collective-permute-start.9 = (bf16[1,96,1536]{2,1,0:T(8,128)(2,1)}, bf16[1,96,1536]{2,1,0:T(8,128)(2,1)}, u32[]{:S(2)}, u32[]{:S(2)}) collective-permute-start(bf16[1,96,1536]{2,1,0:T(8,128)(2,1)} %maximum_bitcast_fusion.2), channel_id=1, source_target_pairs={{0,16},{4,20},{8,24},{12,28},{16,0},{20,4},{24,8},{28,12},{1,17},{... | collective-permute-start | bytes 884744 | tf_op jit(solution)/shard_map/ppermute | solution.py:310
  6.6 1.5 slice_bitcast_fusion.31
  10.5 1.6 collective-permute-start.7
  13.2 13.3 %collective-permute-done.1 = bf16[1,96,768]{2,1,0:T(8,128)(2,1)} collective-permute-done((bf16[1,96,768]{2,1,0:T(8,128)(2,1)}, bf16[1,96,768]{2,1,0:T(8,128)(2,1)}, u32[]{:S(2)}, u32[]{:S(2)}) %collective-permute-start.1) | collective-permute-done | bytes 147488 | tf_op jit(solution)/shard_map/ppermute | solution.py:310
  29.6 1.4 collective-permute-start.10
  30.9 6.7 %collective-permute-done.2 = bf16[2,96,768]{2,1,0:T(8,128)(2,1)S(1)} collective-permute-done((bf16[2,96,768]{2,1,0:T(8,128)(2,1)S(1)}, bf16[2,96,768]{2,1,0:T(8,128)(2,1)S(1)}, u32[]{:S(2)}, u32[]{:S(2)}) %collective-permute-start.2) | collective-permute-done | bytes 294944 | tf_op jit(solution)/shard_map/ppermute | solution.py:310
  37.8 1.6 collective-permute-start.4
  39.7 1.6 collective-permute-start.3
  41.2 3.4 %collective-permute-done.4 = bf16[4,96,384]{2,1,0:T(8,128)(2,1)S(1)} collective-permute-done((bf16[4,96,384]{2,1,0:T(8,128)(2,1)S(1)}, bf16[4,96,384]{2,1,0:T(8,128)(2,1)S(1)}, u32[]{:S(2)}, u32[]{:S(2)}) %collective-permute-start.4) | collective-permute-done | bytes 294944 | tf_op jit(solution)/shard_map/ppermute | solution.py:310
  44.7 1.6 collective-permute-start.5
  46.3 2.2 collective-permute-done.10
  48.8 1.3 collective-permute-start.13
  50.2 8.7 %collective-permute-done.5 = bf16[2,4,96,384]{3,2,1,0:T(8,128)(2,1)S(1)} collective-permute-done((bf16[2,4,96,384]{3,2,1,0:T(8,128)(2,1)S(1)}, bf16[2,4,96,384]{3,2,1,0:T(8,128)(2,1)S(1)}, u32[]{:S(2)}, u32[]{:S(2)}) %collective-permute-start.5) | collective-permute-done | bytes 589856 | tf_op jit(solution)/shard_map/ppermute | solution.py:310
  60.4 4.8 %collective-permute-done.13 = bf16[4,96,768]{2,1,0:T(8,128)(2,1)S(1)} collective-permute-done((bf16[4,96,768]{2,1,0:T(8,128)(2,1)S(1)}, bf16[4,96,768]{2,1,0:T(8,128)(2,1)S(1)}, u32[]{:S(2)}, u32[]{:S(2)}) %collective-permute-start.13) | collective-permute-done | bytes 589856 | tf_op jit(solution)/shard_map/ppermute | solution.py:310
  65.3 1.3 collective-permute-start.14
  66.6 1.6 broadcast_select_fusion.1
  69.9 5.3 %collective-permute-done.6 = bf16[768,384]{1,0:T(8,128)(2,1)S(1)} collective-permute-done((bf16[768,384]{1,0:T(8,128)(2,1)S(1)}, bf16[768,384]{1,0:T(8,128)(2,1)S(1)}, u32[]{:S(2)}, u32[]{:S(2)}) %collective-permute-start.6) | collective-permute-done | bytes 589856 | tf_op jit(solution)/shard_map/ppermute | solution.py:310
  76.1 4.9 %project.1 = (bf16[1024,768]{1,0:T(8,128)(2,1)S(1)}, bf16[1024,576]{1,0:T(8,128)(2,1)S(1)}, bf16[1024,576]{1,0:T(8,128)(2,1)S(1)}) custom-call(bf16[1024,1536]{1,0:T(8,128)(2,1)S(1)} %pad_maximum_fusion.x_ref.cot_ref, f32[1,768]{1,0:T(1,128)S(1)} %reshape.612.gain_ref, f32[1,768]{1,0:T(1,128)S(1)} %reshape.613.bias_ref, ...), custom_call_target="tpu_custom_call" | custom-call | flops 1811939328 | bytes 6291456 | tf_op jit(solution)/shard_map/project/pallas_call | solution.py:58
  81.0 5.4 %attend.2 = (bf16[1024,256]{1,0:T(8,128)(2,1)S(1)}, f32[8,1024]{1,0:T(8,128)S(1)}) custom-call(bf16[1024,576]{1,0:T(8,128)(2,1)S(1)} %get-tuple-element.37.p_ref, s32[1024,1]{1,0:T(8,128)S(1)} %copy-done.8), custom_call_target="tpu_custom_call" | custom-call | flops 805306368 | bytes 2359296 | tf_op jit(solution)/shard_map/attend/pallas_call | solution.py:123
  86.5 5.4 %attend.3 = (bf16[1024,256]{1,0:T(8,128)(2,1)S(1)}, f32[8,1024]{1,0:T(8,128)S(1)}) custom-call(bf16[1024,576]{1,0:T(8,128)(2,1)S(1)} %get-tuple-element.39.p_ref, s32[1024,1]{1,0:T(8,128)S(1)} %copy-done.8), custom_call_target="tpu_custom_call" | custom-call | flops 805306368 | bytes 2359296 | tf_op jit(solution)/shard_map/attend/pallas_call | solution.py:123
  91.9 1.6 select_bitcast_fusion.5
  96.1 10.1 %collective-permute-done.11 = bf16[4,96,768]{2,1,0:T(8,128)(2,1)S(1)} collective-permute-done((bf16[4,96,768]{2,1,0:T(8,128)(2,1)S(1)}, bf16[4,96,768]{2,1,0:T(8,128)(2,1)S(1)}, u32[]{:S(2)}, u32[]{:S(2)}) %collective-permute-start.11) | collective-permute-done | bytes 589856 | tf_op jit(solution)/shard_map/ppermute | solution.py:310
  106.5 1.4 collective-permute-start.12
  108.0 1.3 convert_reduce_fusion
  109.3 1.5 fusion.11
  110.9 1.4 pad_maximum_fusion.7
  113.7 17.4 %collective-permute-done.12.up1_ref = bf16[768,768]{1,0:T(8,128)(2,1)} collective-permute-done((bf16[768,768]{1,0:T(8,128)(2,1)S(1)}, bf16[768,768]{1,0:T(8,128)(2,1)}, u32[]{:S(2)}, u32[]{:S(2)}) %collective-permute-start.12) | collective-permute-done | bytes 1179680 | tf_op jit(solution)/shard_map/ppermute | solution.py:310
  131.1 19.8 %mlp_pass.1 = (f32[1024,768]{1,0:T(8,128)}, bf16[1024,768]{1,0:T(8,128)(2,1)S(1)}, bf16[1024,1536]{1,0:T(8,128)(2,1)}, bf16[1024,1536]{1,0:T(8,128)(2,1)}, bf16[...) custom-call(bf16[1024,1536]{1,0:T(8,128)(2,1)} %copy-done.2, ...), custom_call_target="tpu_custom_call" | custom-call | flops 9663676416 | bytes 23592960 | tf_op jit(solution)/shard_map/mlp_pass/pallas_call | solution.py:239
  150.9 3.0 %fusion.21 = bf16[768,768]{1,0:T(8,128)(2,1)S(1)} fusion(bf16[1024,768]{1,0:T(8,128)(2,1)S(1)} %get-tuple-element.57, bf16[1024,1536]{1,0:T(8,128)(2,1)} %get-tuple-element.58), kind=kOutput, calls=%fused_computation.33 | convolution fusion | flops 1208549376 | bytes 4325376 | tf_op jit(solution)/shard_map/dot_general | solution.py:26
  154.0 1.5 fusion.24
  155.8 1.4 collective-permute-start.29
  158.3 1.4 fusion.30
  159.8 1.5 collective-permute-start.31
  161.9 1.4 fusion.27
  165.0 14.3 %collective-permute-done.29 = bf16[2,4,96,768]{3,2,1,0:T(8,128)(2,1)S(1)} collective-permute-done((bf16[2,4,96,768]{3,2,1,0:T(8,128)(2,1)S(1)}, bf16[2,4,96,768]{3,2,1,0:T(8,128)(2,1)S(1)}, u32[]{:S(2)}, u32[]{:S(2)}) %collective-permute-start.29) | collective-permute-done | bytes 1179680 | tf_op jit(solution)/shard_map/ppermute | solution.py:310
  180.5 1.5 collective-permute-start.30
  182.0 6.8 %collective-permute-done.31 = bf16[768,768]{1,0:T(8,128)(2,1)S(1)} collective-permute-done((bf16[768,768]{1,0:T(8,128)(2,1)S(1)}, bf16[768,768]{1,0:T(8,128)(2,1)S(1)}, u32[]{:S(2)}, u32[]{:S(2)}) %collective-permute-start.31) | collective-permute-done | bytes 1179680 | tf_op jit(solution)/shard_map/ppermute | solution.py:310
  189.9 1.4 collective-permute-start.32
  191.3 5.9 %norm_back.1 = (f32[1024,768]{1,0:T(8,128)S(1)}, bf16[1024,768]{1,0:T(8,128)(2,1)S(1)}, bf16[1024,256]{1,0:T(8,128)(2,1)S(1)}, bf16[1024,256]{1,0:T(8,128)(2,1)S(1)}, f32[8,768]{1,0:T(8,128)S(1)}) custom-call(f32[1024,768]{1,0:T(8,128)S(1)} %copy-done.3, bf16[1024,1536]{1,0:T(8,128)(2,1)} %copy-done.2, bf16[1024,768]{1,0:T(8,128)(2,1)S(1)} %get-tuple-element.43.ga_ref, ...), custom_call_target="tpu_custom_call" | custom-call | flops 805306368 | bytes 15728640 | tf_op jit(solution)/shard_map/norm_back/pallas_call | solution.py:289
  197.3 5.6 %attend_back.2 = (bf16[1024,576]{1,0:T(8,128)(2,1)S(1)}, f32[1,576]{1,0:T(1,128)S(1)}) custom-call(bf16[1024,576]{1,0:T(8,128)(2,1)S(1)} %copy-done.21, s32[1024,1]{1,0:T(8,128)S(1)} %copy-done.9, bf16[1024,256]{1,0:T(8,128)(2,1)S(1)} %copy-done.11, f32[8,1024]{1,0:T(8,128)S(1)} %get-tuple-element.45.log_ref, bf16[1024,256]{1,0:T(8,128)(2,1)S(1)} %get-tuple-element.46.grad_ref), custom_call_target="tpu_custom_call" | custom-call | flops 2013265920 | bytes 4718592 | tf_op jit(solution)/shard_map/attend_back/pallas_call | solution.py:181
  205.6 5.9 %attend_back.3 = (bf16[1024,576]{1,0:T(8,128)(2,1)S(1)}, f32[1,576]{1,0:T(1,128)S(1)}) custom-call(bf16[1024,576]{1,0:T(8,128)(2,1)S(1)} %copy-done.19, s32[1024,1]{1,0:T(8,128)S(1)} %copy-done.9, bf16[1024,256]{1,0:T(8,128)(2,1)S(1)} %copy-done.13, f32[8,1024]{1,0:T(8,128)S(1)} %get-tuple-element.48.log_ref, bf16[1024,256]{1,0:T(8,128)(2,1)S(1)} %get-tuple-element.49.grad_ref), custom_call_target="tpu_custom_call" | custom-call | flops 2013265920 | bytes 4718592 | tf_op jit(solution)/shard_map/attend_back/pallas_call | solution.py:181
  218.5 1.5 collective-permute-start.25
  220.0 1.7 add_convert_fusion.2
  222.9 2.0 fusion.46
  224.8 1.9 fusion.44
  226.8 2.4 convolution_convert_fusion.4
  229.3 1.5 add_convert_fusion.4
  230.8 1.3 fusion.34
  234.2 4.1 %collective-permute-start.33 = (bf16[2,96,1536]{2,1,0:T(8,128)(2,1)}, bf16[2,96,1536]{2,1,0:T(8,128)(2,1)}, u32[]{:S(2)}, u32[]{:S(2)}) collective-permute-start(bf16[2,96,1536]{2,1,0:T(8,128)(2,1)} %select_bitcast_fusion), channel_id=1, source_target_pairs={{0,8},{4,12},{8,0},{12,4},{16,24},{20,28},{24,16},{28,20},{1,9},{5... | collective-permute-start | bytes 1769480 | tf_op jit(solution)/shard_map/ppermute | solution.py:310
  238.2 1.8 fusion.52
  240.5 2.0 add_convert_fusion.5
  242.6 2.1 copy.72
  246.8 4.9 %fusion.10 = (f32[768]{0:T(1024)S(1)}, f32[512]{0:T(512)S(1)}, f32[512]{0:T(512)}, f32[768]{0:T(1024)S(1)}, f32[512,768]{1,0:T(8,128)}) fusion(bf16[512,768]{1,0:T(8,128)(2,1)} %param.15, f32[512]{0:T(512)S(1)} %add_rsqrt_fusion, f32[512]{0:T(512)S(1)} %broadcast_multiply_fusion.2, f32[768]{0:T(1024)S(1)} %copy-done.56, ...), kind=kLoop, calls=%fused_computation.17 | loop fusion | flops 5109248 | bytes 6308864 | tf_op jit(solution)/shard_map/reduce_sum | solution.py:471
  252.5 2.1 fusion.48
  255.6 1.8 select_bitcast_fusion.12
  257.4 4.0 %collective-permute-start.34 = (bf16[1,96,1536]{2,1,0:T(8,128)(2,1)}, bf16[1,96,1536]{2,1,0:T(8,128)(2,1)}, u32[]{:S(2)}, u32[]{:S(2)}) collective-permute-start(bf16[1,96,1536]{2,1,0:T(8,128)(2,1)} %select_bitcast_fusion.12), channel_id=1, source_target_pairs={{0,16},{4,20},{8,24},{12,28},{16,0},{20,4},{24,8},{28,12},{1,17},{... | collective-permute-start | bytes 884744 | tf_op jit(solution)/shard_map/ppermute | solution.py:310
  263.9 2.2 collective-permute-done.20
  266.9 3.2 %fusion.9 = bf16[512,768]{1,0:T(8,128)(2,1)} fusion(bf16[512,768]{1,0:T(8,128)(2,1)} %param.15, f32[1024,768]{1,0:T(8,128)S(1)} %get-tuple-element.44, s32[]{:T(128)S(6)} %select_n.549, f32[512,768]{1,0:T(8,128)} %get-tuple-element.94, f32[512]{0:T(512)S(1)} %get-tuple-element.162, f32[512]{0:T(512)S(1)} %get-tuple-element.163, f32[768]{0:T(1024)S(1)} %copy-done.56, ...), kind=kLoop, calls=%fused_computation.16 | loop fusion | flops 3932160 | bytes 4729860 | tf_op jit(solution)/shard_map/convert_element_type | solution.py:469
  270.1 2.8 collective-permute-done.21
  275.4 2.3 collective-permute-done.22
  280.1 2.0 collective-permute-done.27
  282.3 3.6 %collective-permute-start.28 = (bf16[1,96,768]{2,1,0:T(8,128)(2,1)S(1)}, bf16[1,96,768]{2,1,0:T(8,128)(2,1)S(1)}, u32[]{:S(2)}, u32[]{:S(2)}) collective-permute-start(bf16[1,96,768]{2,1,0:T(8,128)(2,1)S(1)} %select_bitcast_fusion.24), channel_id=1, source_target_pairs={{0,16},{4,20},{8,24},{12,28},{16,0},{20,4},{24,8},{28,12},{1,17},{... | collective-permute-start | bytes 442376 | tf_op jit(solution)/shard_map/ppermute | solution.py:310
  286.7 3.3 %collective-permute-done.28 = bf16[1,96,768]{2,1,0:T(8,128)(2,1)S(1)} collective-permute-done((bf16[1,96,768]{2,1,0:T(8,128)(2,1)S(1)}, bf16[1,96,768]{2,1,0:T(8,128)(2,1)S(1)}, u32[]{:S(2)}, u32[]{:S(2)}) %collective-permute-start.28) | collective-permute-done | bytes 147488 | tf_op jit(solution)/shard_map/ppermute | solution.py:310
  (282 shorter events, 49.7 us)
Async XLA Ops:
  0.6 11.5 %copy-start = (s32[2,1024]{1,0:T(2,128)S(1)}, s32[2,1024]{1,0:T(2,128)}, u32[]{:S(2)}) copy-start(s32[2,1024]{1,0:T(2,128)} %param.16) | copy-start | bytes 24580
  0.7 9.2 %copy-start.22 = (bf16[512,768]{1,0:T(8,128)(2,1)S(1)}, bf16[512,768]{1,0:T(8,128)(2,1)}, u32[]{:S(2)}) copy-start(bf16[512,768]{1,0:T(8,128)(2,1)} %param.15) | copy-start | bytes 2359300
  0.7 9.2 %copy-start.49 = (bf16[512,768]{1,0:T(8,128)(2,1)S(1)}, bf16[512,768]{1,0:T(8,128)(2,1)}, u32[]{:S(2)}) copy-start(bf16[512,768]{1,0:T(8,128)(2,1)} %param.29) | copy-start | bytes 2359300
  2.5 25.9 %collective-permute-start.9 = (bf16[1,96,1536]{2,1,0:T(8,128)(2,1)}, bf16[1,96,1536]{2,1,0:T(8,128)(2,1)}, u32[]{:S(2)}, u32[]{:S(2)}) collective-permute-start(bf16[1,96,1536]{2,1,0:T(8,128)(2,1)} %maximum_bitcast_fusion.2), channel_id=1, source_target_pairs={{0,16},{4,20},{8,24},{12,28},{16,0},{20,4},{24,8},{28,12},{1,17},{... | collective-permute-start | bytes 884744 | tf_op jit(solution)/shard_map/ppermute | solution.py:310
  9.7 16.8 %collective-permute-start.1 = (bf16[1,96,768]{2,1,0:T(8,128)(2,1)}, bf16[1,96,768]{2,1,0:T(8,128)(2,1)}, u32[]{:S(2)}, u32[]{:S(2)}) collective-permute-start(bf16[1,96,768]{2,1,0:T(8,128)(2,1)} %maximum_bitcast_fusion.3), channel_id=1, source_target_pairs={{0,16},{4,20},{8,24},{12,28},{16,0},{20,4},{24,8},{28,12},{1,17},{... | collective-permute-start | bytes 442376 | tf_op jit(solution)/shard_map/ppermute | solution.py:310
  9.9 18.5 %copy-start.52 = (bf16[768,96]{0,1:T(8,128)(2,1)S(1)}, bf16[768,96]{0,1:T(8,128)(2,1)}, u32[]{:S(2)}) copy-start(bf16[768,96]{0,1:T(8,128)(2,1)} %param.27) | copy-start | bytes 442372
  9.9 18.5 %copy-start.53 = (bf16[96,768]{1,0:T(8,128)(2,1)S(1)}, bf16[96,768]{1,0:T(8,128)(2,1)}, u32[]{:S(2)}) copy-start(bf16[96,768]{1,0:T(8,128)(2,1)} %param.25) | copy-start | bytes 442372
  10.0 56.6 %collective-permute-start = (bf16[512,1536]{1,0:T(8,128)(2,1)S(1)}, bf16[512,1536]{1,0:T(8,128)(2,1)}, u32[]{:S(2)}, u32[]{:S(2)}) collective-permute-start(bf16[512,1536]{1,0:T(8,128)(2,1)S(1)} %constant_dynamic-update-slice_fusion), channel_id=1, source_target_pairs={{0,1},{1,0},{2,3},{3,2},{4,5},{5,4},{6,7},{7,6},{8,9},{9,8},{10,11... | collective-permute-start | bytes 4718600 | tf_op jit(solution)/shard_map/ppermute | solution.py:310
  10.5 29.0 %collective-permute-start.7 = (f32[1152]{0:T(1024)S(1)}, f32[1152]{0:T(1024)S(1)}, u32[]{:S(2)}, u32[]{:S(2)}) collective-permute-start(f32[1152]{0:T(1024)S(1)} %pad_maximum_fusion.21), channel_id=1, source_target_pairs={{0,2},{1,3},{2,0},{3,1},{4,6},{5,7},{6,4},{7,5},{8,10},{9,11},{10,... | collective-permute-start | bytes 13832 | tf_op jit(solution)/shard_map/ppermute | solution.py:310
  27.6 10.0 %collective-permute-start.2 = (bf16[2,96,768]{2,1,0:T(8,128)(2,1)S(1)}, bf16[2,96,768]{2,1,0:T(8,128)(2,1)S(1)}, u32[]{:S(2)}, u32[]{:S(2)}) collective-permute-start(bf16[2,96,768]{2,1,0:T(8,128)(2,1)S(1)} %maximum_bitcast_fusion.1), channel_id=1, source_target_pairs={{0,8},{4,12},{8,0},{12,4},{16,24},{20,28},{24,16},{28,20},{1,9},{5... | collective-permute-start | bytes 884744 | tf_op jit(solution)/shard_map/ppermute | solution.py:310
  29.6 19.0 %collective-permute-start.10 = (bf16[2,96,1536]{2,1,0:T(8,128)(2,1)S(1)}, bf16[2,96,1536]{2,1,0:T(8,128)(2,1)S(1)}, u32[]{:S(2)}, u32[]{:S(2)}) collective-permute-start(bf16[2,96,1536]{2,1,0:T(8,128)(2,1)S(1)} %maximum_bitcast_fusion), channel_id=1, source_target_pairs={{0,8},{4,12},{8,0},{12,4},{16,24},{20,28},{24,16},{28,20},{1,9},{5... | collective-permute-start | bytes 1769480 | tf_op jit(solution)/shard_map/ppermute | solution.py:310
  37.8 6.8 %collective-permute-start.4 = (bf16[4,96,384]{2,1,0:T(8,128)(2,1)S(1)}, bf16[4,96,384]{2,1,0:T(8,128)(2,1)S(1)}, u32[]{:S(2)}, u32[]{:S(2)}) collective-permute-start(bf16[4,96,384]{2,1,0:T(8,128)(2,1)S(1)} %get-tuple-element.126), channel_id=1, source_target_pairs={{0,2},{1,3},{2,0},{3,1},{4,6},{5,7},{6,4},{7,5},{8,10},{9,11},{10,... | collective-permute-start | bytes 884744 | tf_op jit(solution)/shard_map/ppermute | solution.py:310
  39.7 10.5 %collective-permute-start.3 = (bf16[4,96,384]{2,1,0:T(8,128)(2,1)S(1)}, bf16[4,96,384]{2,1,0:T(8,128)(2,1)S(1)}, u32[]{:S(2)}, u32[]{:S(2)}) collective-permute-start(bf16[4,96,384]{2,1,0:T(8,128)(2,1)S(1)} %get-tuple-element.124), channel_id=1, source_target_pairs={{0,4},{4,0},{8,12},{12,8},{16,20},{20,16},{24,28},{28,24},{1,5},{5... | collective-permute-start | bytes 884744 | tf_op jit(solution)/shard_map/ppermute | solution.py:310
  44.7 14.2 %collective-permute-start.5 = (bf16[2,4,96,384]{3,2,1,0:T(8,128)(2,1)S(1)}, bf16[2,4,96,384]{3,2,1,0:T(8,128)(2,1)S(1)}, u32[]{:S(2)}, u32[]{:S(2)}) collective-permute-start(bf16[2,4,96,384]{3,2,1,0:T(8,128)(2,1)S(1)} %pad_maximum_fusion.12), channel_id=1, source_target_pairs={{0,4},{4,0},{8,12},{12,8},{16,20},{20,16},{24,28},{28,24},{1,5},{5... | collective-permute-start | bytes 1769480 | tf_op jit(solution)/shard_map/ppermute | solution.py:310
  48.8 16.3 %collective-permute-start.13 = (bf16[4,96,768]{2,1,0:T(8,128)(2,1)S(1)}, bf16[4,96,768]{2,1,0:T(8,128)(2,1)S(1)}, u32[]{:S(2)}, u32[]{:S(2)}) collective-permute-start(bf16[4,96,768]{2,1,0:T(8,128)(2,1)S(1)} %get-tuple-element.107), channel_id=1, source_target_pairs={{0,2},{1,3},{2,0},{3,1},{4,6},{5,7},{6,4},{7,5},{8,10},{9,11},{10,... | collective-permute-start | bytes 1769480 | tf_op jit(solution)/shard_map/ppermute | solution.py:310
  59.3 36.1 %copy-start.35 = (bf16[4,2,96,384]{3,2,1,0:T(8,128)(2,1)}, bf16[4,2,96,384]{3,2,1,0:T(8,128)(2,1)S(1)}, u32[]{:S(2)}) copy-start(bf16[4,2,96,384]{3,2,1,0:T(8,128)(2,1)S(1)} %copy.59) | copy-start | bytes 1769476
  59.4 15.7 %collective-permute-start.6 = (bf16[768,384]{1,0:T(8,128)(2,1)S(1)}, bf16[768,384]{1,0:T(8,128)(2,1)S(1)}, u32[]{:S(2)}, u32[]{:S(2)}) collective-permute-start(bf16[768,384]{1,0:T(8,128)(2,1)S(1)} %bitcast.359), channel_id=1, source_target_pairs={{0,2},{1,3},{2,0},{3,1},{4,6},{5,7},{6,4},{7,5},{8,10},{9,11},{10,... | collective-permute-start | bytes 1769480 | tf_op jit(solution)/shard_map/ppermute | solution.py:310
  60.2 34.5 %copy-start.37 = (bf16[4,2,96,384]{3,2,1,0:T(8,128)(2,1)}, bf16[4,2,96,384]{3,2,1,0:T(8,128)(2,1)S(1)}, u32[]{:S(2)}) copy-start(bf16[4,2,96,384]{3,2,1,0:T(8,128)(2,1)S(1)} %copy.58) | copy-start | bytes 1769476
  60.4 15.7 %copy-start.4 = (bf16[768,768]{1,0:T(8,128)(2,1)}, bf16[768,768]{1,0:T(8,128)(2,1)S(1)}, u32[]{:S(2)}) copy-start(bf16[768,768]{1,0:T(8,128)(2,1)S(1)} %pad_maximum_fusion.1.w0_ref) | copy-start | bytes 3538948
  65.3 26.6 %collective-permute-start.14 = (bf16[2,4,96,768]{3,2,1,0:T(8,128)(2,1)S(1)}, bf16[2,4,96,768]{3,2,1,0:T(8,128)(2,1)S(1)}, u32[]{:S(2)}, u32[]{:S(2)}) collective-permute-start(bf16[2,4,96,768]{3,2,1,0:T(8,128)(2,1)S(1)} %pad_maximum_fusion.5), channel_id=1, source_target_pairs={{0,4},{4,0},{8,12},{12,8},{16,20},{20,16},{24,28},{28,24},{1,5},{5... | collective-permute-start | bytes 3538952 | tf_op jit(solution)/shard_map/ppermute | solution.py:310
  69.9 11.1 %copy-start.2 = (bf16[1024,1536]{1,0:T(8,128)(2,1)}, bf16[1024,1536]{1,0:T(8,128)(2,1)S(1)}, u32[]{:S(2)}) copy-start(bf16[1024,1536]{1,0:T(8,128)(2,1)S(1)} %pad_maximum_fusion.x_ref.cot_ref) | copy-start | bytes 9437188
  69.9 6.2 %copy-start.15 = (f32[1,576]{1,0:T(1,128)S(1)}, f32[1,576]{1,0:T(1,128)}, u32[]{:S(2)}) copy-start(f32[1,576]{1,0:T(1,128)} %constant.168.clone.1.scale_ref) | copy-start | bytes 6916
  76.1 4.9 %copy-start.6 = (bf16[768,768]{1,0:T(8,128)(2,1)}, bf16[768,768]{1,0:T(8,128)(2,1)S(1)}, u32[]{:S(2)}) copy-start(bf16[768,768]{1,0:T(8,128)(2,1)S(1)} %pad_maximum_fusion.2.w1_ref) | copy-start | bytes 3538948
  76.1 4.9 %copy-start.8 = (s32[1024,1]{1,0:T(8,128)S(1)}, s32[1024,1]{1,0:T(8,128)}, u32[]{:S(2)}) copy-start(s32[1024,1]{1,0:T(8,128)} %copy.60.seg_ref) | copy-start | bytes 12292
  81.0 5.5 %copy-start.16 = (bf16[1024,768]{1,0:T(8,128)(2,1)}, bf16[1024,768]{1,0:T(8,128)(2,1)S(1)}, u32[]{:S(2)}) copy-start(bf16[1024,768]{1,0:T(8,128)(2,1)S(1)} %get-tuple-element.55) | copy-start | bytes 4718596
  81.0 5.5 %copy-start.20 = (bf16[1024,576]{1,0:T(8,128)(2,1)}, bf16[1024,576]{1,0:T(8,128)(2,1)S(1)}, u32[]{:S(2)}) copy-start(bf16[1024,576]{1,0:T(8,128)(2,1)S(1)} %get-tuple-element.37.p_ref) | copy-start | bytes 3538948
  81.0 5.5 %copy-start.18 = (bf16[1024,576]{1,0:T(8,128)(2,1)}, bf16[1024,576]{1,0:T(8,128)(2,1)S(1)}, u32[]{:S(2)}) copy-start(bf16[1024,576]{1,0:T(8,128)(2,1)S(1)} %get-tuple-element.39.p_ref) | copy-start | bytes 3538948
  86.4 8.3 %copy-start.10 = (bf16[1024,256]{1,0:T(8,128)(2,1)}, bf16[1024,256]{1,0:T(8,128)(2,1)S(1)}, u32[]{:S(2)}) copy-start(bf16[1024,256]{1,0:T(8,128)(2,1)S(1)} %get-tuple-element.38.out_ref) | copy-start | bytes 1572868
  93.5 12.7 %collective-permute-start.11 = (bf16[4,96,768]{2,1,0:T(8,128)(2,1)S(1)}, bf16[4,96,768]{2,1,0:T(8,128)(2,1)S(1)}, u32[]{:S(2)}, u32[]{:S(2)}) collective-permute-start(bf16[4,96,768]{2,1,0:T(8,128)(2,1)S(1)} %get-tuple-element.105), channel_id=1, source_target_pairs={{0,4},{4,0},{8,12},{12,8},{16,20},{20,16},{24,28},{28,24},{1,5},{5... | collective-permute-start | bytes 1769480 | tf_op jit(solution)/shard_map/ppermute | solution.py:310
  96.0 17.7 %collective-permute-start.8 = (bf16[1024,768]{1,0:T(8,128)(2,1)S(1)}, bf16[1024,768]{1,0:T(8,128)(2,1)}, u32[]{:S(2)}, u32[]{:S(2)}) collective-permute-start(bf16[1024,768]{1,0:T(8,128)(2,1)S(1)} %add_convert_fusion.pa_ref), channel_id=1, source_target_pairs={{0,1},{1,0},{2,3},{3,2},{4,5},{5,4},{6,7},{7,6},{8,9},{9,8},{10,11... | collective-permute-start | bytes 4718600 | tf_op jit(solution)/shard_map/ppermute | solution.py:310
  106.5 24.5 %collective-permute-start.12 = (bf16[768,768]{1,0:T(8,128)(2,1)S(1)}, bf16[768,768]{1,0:T(8,128)(2,1)}, u32[]{:S(2)}, u32[]{:S(2)}) collective-permute-start(bf16[768,768]{1,0:T(8,128)(2,1)S(1)} %bitcast.329), channel_id=1, source_target_pairs={{0,2},{1,3},{2,0},{3,1},{4,6},{5,7},{6,4},{7,5},{8,10},{9,11},{10,... | collective-permute-start | bytes 3538952 | tf_op jit(solution)/shard_map/ppermute | solution.py:310
  155.8 23.5 %collective-permute-start.29 = (bf16[2,4,96,768]{3,2,1,0:T(8,128)(2,1)S(1)}, bf16[2,4,96,768]{3,2,1,0:T(8,128)(2,1)S(1)}, u32[]{:S(2)}, u32[]{:S(2)}) collective-permute-start(bf16[2,4,96,768]{3,2,1,0:T(8,128)(2,1)S(1)} %pad_maximum_fusion.8), channel_id=1, source_target_pairs={{0,4},{4,0},{8,12},{12,8},{16,20},{20,16},{24,28},{28,24},{1,5},{5... | collective-permute-start | bytes 3538952 | tf_op jit(solution)/shard_map/ppermute | solution.py:310
  157.3 6.1 %collective-permute-start.15 = (bf16[512,768]{1,0:T(8,128)(2,1)S(1)}, bf16[512,768]{1,0:T(8,128)(2,1)S(1)}, u32[]{:S(2)}, u32[]{:S(2)}) collective-permute-start(bf16[512,768]{1,0:T(8,128)(2,1)S(1)} %constant_dynamic-slice_fusion), channel_id=1, source_target_pairs={{0,1},{1,0},{2,3},{3,2},{4,5},{5,4},{6,7},{7,6},{8,9},{9,8},{10,11... | collective-permute-start | bytes 2359304 | tf_op jit(solution)/shard_map/ppermute | solution.py:310
  159.8 29.0 %collective-permute-start.31 = (bf16[768,768]{1,0:T(8,128)(2,1)S(1)}, bf16[768,768]{1,0:T(8,128)(2,1)S(1)}, u32[]{:S(2)}, u32[]{:S(2)}) collective-permute-start(bf16[768,768]{1,0:T(8,128)(2,1)S(1)} %fusion.30), channel_id=1, source_target_pairs={{0,2},{1,3},{2,0},{3,1},{4,6},{5,7},{6,4},{7,5},{8,10},{9,11},{10,... | collective-permute-start | bytes 3538952 | tf_op jit(solution)/shard_map/ppermute | solution.py:310
  161.2 30.1 %collective-permute-start.16 = (bf16[1024,768]{1,0:T(8,128)(2,1)S(1)}, bf16[1024,768]{1,0:T(8,128)(2,1)S(1)}, u32[]{:S(2)}, u32[]{:S(2)}) collective-permute-start(bf16[1024,768]{1,0:T(8,128)(2,1)S(1)} %get-tuple-element.43.ga_ref), channel_id=1, source_target_pairs={{0,1},{1,0},{2,3},{3,2},{4,5},{5,4},{6,7},{7,6},{8,9},{9,8},{10,11... | collective-permute-start | bytes 4718600 | tf_op jit(solution)/shard_map/ppermute | solution.py:310
  179.3 9.7 %copy-start.47 = (bf16[2,4,96,768]{3,2,1,0:T(8,128)(2,1)}, bf16[2,4,96,768]{3,2,1,0:T(8,128)(2,1)S(1)}, u32[]{:S(2)}) copy-start(bf16[2,4,96,768]{3,2,1,0:T(8,128)(2,1)S(1)} %collective-permute-done.29) | copy-start | bytes 3538948
  180.5 48.7 %collective-permute-start.30 = (bf16[4,96,768]{2,1,0:T(8,128)(2,1)}, bf16[4,96,768]{2,1,0:T(8,128)(2,1)}, u32[]{:S(2)}, u32[]{:S(2)}) collective-permute-start(bf16[4,96,768]{2,1,0:T(8,128)(2,1)} %fusion.35), channel_id=1, source_target_pairs={{0,2},{1,3},{2,0},{3,1},{4,6},{5,7},{6,4},{7,5},{8,10},{9,11},{10,... | collective-permute-start | bytes 1769480 | tf_op jit(solution)/shard_map/ppermute | solution.py:310
  189.9 7.3 %copy-start.9 = (s32[1024,1]{1,0:T(8,128)S(1)}, s32[1024,1]{1,0:T(8,128)}, u32[]{:S(2)}) copy-start(s32[1024,1]{1,0:T(8,128)} %copy.60.seg_ref) | copy-start | bytes 12292
  189.9 7.3 %copy-start.11 = (bf16[1024,256]{1,0:T(8,128)(2,1)S(1)}, bf16[1024,256]{1,0:T(8,128)(2,1)}, u32[]{:S(2)}) copy-start(bf16[1024,256]{1,0:T(8,128)(2,1)} %copy-done.10) | copy-start | bytes 1572868
  189.9 7.3 %copy-start.21 = (bf16[1024,576]{1,0:T(8,128)(2,1)S(1)}, bf16[1024,576]{1,0:T(8,128)(2,1)}, u32[]{:S(2)}) copy-start(bf16[1024,576]{1,0:T(8,128)(2,1)} %copy-done.20) | copy-start | bytes 3538948
  189.9 40.8 %collective-permute-start.32 = (bf16[4,96,768]{2,1,0:T(8,128)(2,1)}, bf16[4,96,768]{2,1,0:T(8,128)(2,1)}, u32[]{:S(2)}, u32[]{:S(2)}) collective-permute-start(bf16[4,96,768]{2,1,0:T(8,128)(2,1)} %select_bitcast_fusion.1), channel_id=1, source_target_pairs={{0,4},{4,0},{8,12},{12,8},{16,20},{20,16},{24,28},{28,24},{1,5},{5... | collective-permute-start | bytes 1769480 | tf_op jit(solution)/shard_map/ppermute | solution.py:310
  197.2 19.7 %copy-start.14 = (bf16[1024,768]{1,0:T(8,128)(2,1)}, bf16[1024,768]{1,0:T(8,128)(2,1)S(1)}, u32[]{:S(2)}) copy-start(bf16[1024,768]{1,0:T(8,128)(2,1)S(1)} %get-tuple-element.56) | copy-start | bytes 4718596
  197.2 5.7 %copy-start.17 = (bf16[1024,768]{1,0:T(8,128)(2,1)S(1)}, bf16[1024,768]{1,0:T(8,128)(2,1)}, u32[]{:S(2)}) copy-start(bf16[1024,768]{1,0:T(8,128)(2,1)} %copy-done.16) | copy-start | bytes 4718596
  203.9 10.9 %copy-start.43 = (bf16[768,384]{1,0:T(8,128)(2,1)}, bf16[768,384]{1,0:T(8,128)(2,1)S(1)}, u32[]{:S(2)}) copy-start(bf16[768,384]{1,0:T(8,128)(2,1)S(1)} %convolution_convert_fusion.1) | copy-start | bytes 1769476
  215.8 22.4 %collective-permute-start.23 = (bf16[2,4,96,384]{3,2,1,0:T(8,128)(2,1)}, bf16[2,4,96,384]{3,2,1,0:T(8,128)(2,1)}, u32[]{:S(2)}, u32[]{:S(2)}) collective-permute-start(bf16[2,4,96,384]{3,2,1,0:T(8,128)(2,1)} %pad_maximum_fusion.15), channel_id=1, source_target_pairs={{0,4},{4,0},{8,12},{12,8},{16,20},{20,16},{24,28},{28,24},{1,5},{5... | collective-permute-start | bytes 1769480 | tf_op jit(solution)/shard_map/ppermute | solution.py:310
  218.5 22.0 %collective-permute-start.25 = (bf16[768,384]{0,1:T(8,128)(2,1)}, bf16[768,384]{0,1:T(8,128)(2,1)}, u32[]{:S(2)}, u32[]{:S(2)}) collective-permute-start(bf16[768,384]{0,1:T(8,128)(2,1)} %pad_maximum_fusion.16), channel_id=1, source_target_pairs={{0,2},{1,3},{2,0},{3,1},{4,6},{5,7},{6,4},{7,5},{8,10},{9,11},{10,... | collective-permute-start | bytes 1769480 | tf_op jit(solution)/shard_map/ppermute | solution.py:310
  221.7 25.1 %collective-permute-start.17 = (bf16[512,768]{1,0:T(8,128)(2,1)}, bf16[512,768]{1,0:T(8,128)(2,1)}, u32[]{:S(2)}, u32[]{:S(2)}) collective-permute-start(bf16[512,768]{1,0:T(8,128)(2,1)} %add_convert_fusion.2), channel_id=1, source_target_pairs={{0,1},{1,0},{2,3},{3,2},{4,5},{5,4},{6,7},{7,6},{8,9},{9,8},{10,11... | collective-permute-start | bytes 2359304 | tf_op jit(solution)/shard_map/ppermute | solution.py:310
  232.1 6.1 %copy-start.46 = (bf16[768,384]{1,0:T(8,128)(2,1)S(1)}, bf16[768,384]{1,0:T(8,128)(2,1)}, u32[]{:S(2)}) copy-start(bf16[768,384]{1,0:T(8,128)(2,1)} %copy-done.45) | copy-start | bytes 1769476
  234.2 18.4 %collective-permute-start.33 = (bf16[2,96,1536]{2,1,0:T(8,128)(2,1)}, bf16[2,96,1536]{2,1,0:T(8,128)(2,1)}, u32[]{:S(2)}, u32[]{:S(2)}) collective-permute-start(bf16[2,96,1536]{2,1,0:T(8,128)(2,1)} %select_bitcast_fusion), channel_id=1, source_target_pairs={{0,8},{4,12},{8,0},{12,4},{16,24},{20,28},{24,16},{28,20},{1,9},{5... | collective-permute-start | bytes 1769480 | tf_op jit(solution)/shard_map/ppermute | solution.py:310
  240.0 6.8 %copy-start.56 = (f32[768]{0:T(1024)S(1)}, f32[768]{0:T(1024)}, u32[]{:S(2)}) copy-start(f32[768]{0:T(1024)} %param.17) | copy-start | bytes 9220
  240.0 32.8 %collective-permute-start.24 = (bf16[4,96,384]{2,1,0:T(8,128)(2,1)}, bf16[4,96,384]{2,1,0:T(8,128)(2,1)}, u32[]{:S(2)}, u32[]{:S(2)}) collective-permute-start(bf16[4,96,384]{2,1,0:T(8,128)(2,1)} %fusion.52), channel_id=1, source_target_pairs={{0,2},{1,3},{2,0},{3,1},{4,6},{5,7},{6,4},{7,5},{8,10},{9,11},{10,... | collective-permute-start | bytes 884744 | tf_op jit(solution)/shard_map/ppermute | solution.py:310
  245.8 6.8 %copy-start.26 = (bf16[4,96,1536]{2,1,0:T(8,128)(2,1)S(1)}, bf16[4,96,1536]{2,1,0:T(8,128)(2,1)}, u32[]{:S(2)}) copy-start(bf16[4,96,1536]{2,1,0:T(8,128)(2,1)} %copy-done.25) | copy-start | bytes 3538948
  245.8 28.3 %collective-permute-start.26 = (bf16[4,96,384]{2,1,0:T(8,128)(2,1)S(1)}, bf16[4,96,384]{2,1,0:T(8,128)(2,1)}, u32[]{:S(2)}, u32[]{:S(2)}) collective-permute-start(bf16[4,96,384]{2,1,0:T(8,128)(2,1)S(1)} %fusion.61), channel_id=1, source_target_pairs={{0,4},{4,0},{8,12},{12,8},{16,20},{20,16},{24,28},{28,24},{1,5},{5... | collective-permute-start | bytes 884744 | tf_op jit(solution)/shard_map/ppermute | solution.py:310
  251.7 9.7 %copy-start.57 = (f32[768]{0:T(1024)S(1)}, f32[768]{0:T(1024)}, u32[]{:S(2)}) copy-start(f32[768]{0:T(1024)} %get-tuple-element.93) | copy-start | bytes 9220
  251.8 2.9 collective-permute-start.18
  254.8 7.4 %collective-permute-start.19 = (f32[5760]{0:T(1024)S(1)}, f32[5760]{0:T(1024)S(1)}, u32[]{:S(2)}, u32[]{:S(2)}) collective-permute-start(f32[5760]{0:T(1024)S(1)} %concatenate.150), channel_id=1, source_target_pairs={{0,2},{1,3},{2,0},{3,1},{4,6},{5,7},{6,4},{7,5},{8,10},{9,11},{10,... | collective-permute-start | bytes 69128 | tf_op jit(solution)/shard_map/ppermute | solution.py:310
  257.4 21.5 %collective-permute-start.34 = (bf16[1,96,1536]{2,1,0:T(8,128)(2,1)}, bf16[1,96,1536]{2,1,0:T(8,128)(2,1)}, u32[]{:S(2)}, u32[]{:S(2)}) collective-permute-start(bf16[1,96,1536]{2,1,0:T(8,128)(2,1)} %select_bitcast_fusion.12), channel_id=1, source_target_pairs={{0,16},{4,20},{8,24},{12,28},{16,0},{20,4},{24,8},{28,12},{1,17},{... | collective-permute-start | bytes 884744 | tf_op jit(solution)/shard_map/ppermute | solution.py:310
  262.2 3.9 %collective-permute-start.20 = (f32[5760]{0:T(1024)S(1)}, f32[5760]{0:T(1024)S(1)}, u32[]{:S(2)}, u32[]{:S(2)}) collective-permute-start(f32[5760]{0:T(1024)S(1)} %add.169), channel_id=1, source_target_pairs={{0,4},{4,0},{8,12},{12,8},{16,20},{20,16},{24,28},{28,24},{1,5},{5... | collective-permute-start | bytes 69128 | tf_op jit(solution)/shard_map/ppermute | solution.py:310
  266.1 6.7 %collective-permute-start.21 = (f32[5760]{0:T(1024)S(1)}, f32[5760]{0:T(1024)S(1)}, u32[]{:S(2)}, u32[]{:S(2)}) collective-permute-start(f32[5760]{0:T(1024)S(1)} %add.170), channel_id=1, source_target_pairs={{0,8},{4,12},{8,0},{12,4},{16,24},{20,28},{24,16},{28,20},{1,9},{5... | collective-permute-start | bytes 69128 | tf_op jit(solution)/shard_map/ppermute | solution.py:310
  266.9 5.9 %copy-start.44 = (bf16[768,384]{1,0:T(8,128)(2,1)S(1)}, bf16[768,384]{1,0:T(8,128)(2,1)}, u32[]{:S(2)}) copy-start(bf16[768,384]{1,0:T(8,128)(2,1)} %copy-done.43) | copy-start | bytes 1769476
  272.8 4.8 %collective-permute-start.22 = (f32[5760]{0:T(1024)S(1)}, f32[5760]{0:T(1024)S(1)}, u32[]{:S(2)}, u32[]{:S(2)}) collective-permute-start(f32[5760]{0:T(1024)S(1)} %add.171), channel_id=1, source_target_pairs={{0,16},{4,20},{8,24},{12,28},{16,0},{20,4},{24,8},{28,12},{1,17},{... | collective-permute-start | bytes 69128 | tf_op jit(solution)/shard_map/ppermute | solution.py:310
  275.3 6.8 %collective-permute-start.27 = (bf16[2,96,768]{2,1,0:T(8,128)(2,1)S(1)}, bf16[2,96,768]{2,1,0:T(8,128)(2,1)S(1)}, u32[]{:S(2)}, u32[]{:S(2)}) collective-permute-start(bf16[2,96,768]{2,1,0:T(8,128)(2,1)S(1)} %select_bitcast_fusion.13), channel_id=1, source_target_pairs={{0,8},{4,12},{8,0},{12,4},{16,24},{20,28},{24,16},{28,20},{1,9},{5... | collective-permute-start | bytes 884744 | tf_op jit(solution)/shard_map/ppermute | solution.py:310
  282.2 9.5 %copy-start.1 = (s32[2,1024]{1,0:T(2,128)S(1)}, s32[2,1024]{1,0:T(2,128)}, u32[]{:S(2)}) copy-start(s32[2,1024]{1,0:T(2,128)} %param.16) | copy-start | bytes 24580
  282.3 7.8 %collective-permute-start.28 = (bf16[1,96,768]{2,1,0:T(8,128)(2,1)S(1)}, bf16[1,96,768]{2,1,0:T(8,128)(2,1)S(1)}, u32[]{:S(2)}, u32[]{:S(2)}) collective-permute-start(bf16[1,96,768]{2,1,0:T(8,128)(2,1)S(1)} %select_bitcast_fusion.24), channel_id=1, source_target_pairs={{0,16},{4,20},{8,24},{12,28},{16,0},{20,4},{24,8},{28,12},{1,17},{... | collective-permute-start | bytes 442376 | tf_op jit(solution)/shard_map/ppermute | solution.py:310
  (40 other events, 79.6 us)
